TPU v7x, 32 devices: a whole 2x2x4 slice. The times are simulated.
32 devices in a mesh: dp: 4 (over x, core), ctx: 8 (over z, y).
Axes of the slice: x: 2, y: 2, z: 4, core: 2. Of those that a mesh axis runs over, the one named last changes fastest.
Arguments:
- query: bfloat16 [4, 2048, 1024], P('dp', 'ctx'), may hold values from -150 to 150
- key: bfloat16 [4, 2048, 1024], P('dp', 'ctx'), may hold values from -3 to 3
- value: bfloat16 [4, 2048, 1024], P('dp', 'ctx'), may hold values from -6 to 6
- grad_out: bfloat16 [4, 2048, 1024], P('dp', 'ctx'), may hold values from -30 to 30
- clause: int32 [4, 2048], P('dp', 'ctx'), may hold values from 0 to 127, never falling along the last dimension, each value on 1 to 48 neighbouring positions
- bias_table: float32 [32, 2], replicated, may hold values from -1.5 to 1.5
Outputs:
- attended: bfloat16 [4, 2048, 1024], P('dp', 'ctx')
- query_gradient: bfloat16 [4, 2048, 1024], P('dp', 'ctx')
- key_gradient: bfloat16 [4, 2048, 1024], P('dp', 'ctx')
- value_gradient: bfloat16 [4, 2048, 1024], P('dp', 'ctx')
- bias_grad: float32 [32, 2], replicated
Inputs may be any that keep to these rules, and one draw needn't show every extreme that they name: Clause ids never fall along a document; a clause holds 1 to 48 tokens, and some clause holds exactly 48.
All inputs are finite; a program needn't handle non-finite values.
Results may differ from a plain program's by a relative error of at most 0.009.
Values may be sent and summed in bfloat16 or wider, within the bound.
A program may use at most 128 MiB of HBM per device.

v0:
```python
import jax
import jax.numpy as jnp
from jax import lax
from jax.sharding import PartitionSpec as P

HEADS = 8
WINDOW = 512
BUCKETS = 32
DILATION_FIRST = 1
DILATION_SECOND = 8
DILATION_THIRD = 32


def swapped(block, axis, bit):
    count = lax.axis_size(axis)
    route = []
    for low in range(count):
        high = low | 1 << bit
        if high != low and high < count:
            route += [(low, high), (high, low)]
    return lax.ppermute(block, axis, route)


def shifted(value, axis, steps):
    count = lax.axis_size(axis)
    leading, last = (max(0, -steps), min(count, count - steps))
    return lax.ppermute(value, axis, [(source, source + steps) for source in range(leading, last)])


def with_halo(shard, sides, width):
    for axis, dim in sides:
        size, length = (lax.axis_size(axis), shard.shape[dim])
        up = [(i, (i + 1) % size) for i in range(size - 1)]
        down = [(j, i) for i, j in up]
        last = lax.slice_in_dim(shard, length - width, length, axis=dim)
        leading = lax.slice_in_dim(shard, 0, width, axis=dim)
        before = lax.ppermute(last, axis, up)
        after = lax.ppermute(leading, axis, down)
        shard = jnp.concatenate([before, shard, after], axis=dim)
    return shard


def sample_rows(matrix, initial_flag, dilation_rate):
    count = matrix.shape[0] // dilation_rate
    head_dim = matrix.shape[1] // HEADS
    grid = matrix.reshape(count, dilation_rate, HEADS, head_dim)
    return jnp.concatenate(
        [grid[:, 0, initial_flag], grid[:, dilation_rate // 2, initial_flag + 1]], axis=1
    )


def spread_rows(sampled, dilation_rate):
    count = sampled.shape[0]
    grid = jnp.zeros((count, dilation_rate) + sampled.shape[1:], sampled.dtype)
    grid = grid.at[:, 0, 0].set(sampled[:, 0]).at[:, dilation_rate // 2, 1].set(sampled[:, 1])
    return grid.reshape((count * dilation_rate,) + sampled.shape[1:])


def upper_half(bit):
    index = lax.axis_index("ctx")
    return index // 2**bit % 2 == 1


def double_rows(block, bits):
    for bit in range(bits):
        other = swapped(block, "ctx", bit)
        block = jnp.where(
            upper_half(bit),
            jnp.concatenate([other, block], axis=0),
            jnp.concatenate([block, other], axis=0),
        )
    return block


def halve_sums(block, bits):
    for bit in reversed(range(bits)):
        half = block.shape[0] // 2
        lower, higher = (block[:half], block[half:])
        upper = upper_half(bit)
        outgoing = jnp.where(upper, lower, higher)
        staying = jnp.where(upper, higher, lower)
        block = staying + swapped(outgoing.astype(jnp.bfloat16), "ctx", bit).astype(outgoing.dtype)
    return block


def span_rows(block, bits):
    return double_rows(block, bits)


def span_sums(block, bits):
    return halve_sums(block, bits)


def rows_side(score_matrix, every_key_rows, every_value_rows, gradient_list, score_scale):
    top = jnp.max(score_matrix, axis=-1, keepdims=True)
    raised = jnp.exp(score_matrix - top)
    totals = jnp.sum(raised, axis=-1, keepdims=True)
    shares = raised / totals
    softmax_weights = shares.astype(jnp.bfloat16)
    attended = jnp.einsum(
        "ezb,beo->zeo", softmax_weights, every_value_rows, preferred_element_type=jnp.float32
    )
    weight_gradient = jnp.einsum(
        "wvx,yvx->vwy", gradient_list, every_value_rows, preferred_element_type=jnp.float32
    )
    delta = jnp.sum(shares * weight_gradient, axis=-1, keepdims=True)
    logit_grads = shares * (weight_gradient - delta)
    score_gradient = logit_grads.astype(jnp.bfloat16)
    query_gradient = (
        jnp.einsum(
            "ezb,beo->zeo", score_gradient, every_key_rows, preferred_element_type=jnp.float32
        )
        * score_scale
    )
    return (
        attended,
        query_gradient,
        softmax_weights,
        score_gradient,
        logit_grads,
        top,
        totals,
        delta,
    )


def keys_side(softmax_weights, score_gradient, query_matrix, gradient_list, score_scale):
    key_gradient = (
        jnp.einsum("vjb,jvw->bvw", score_gradient, query_matrix, preferred_element_type=jnp.float32)
        * score_scale
    )
    value_gradient = jnp.einsum(
        "vjb,jvw->bvw", softmax_weights, gradient_list, preferred_element_type=jnp.float32
    )
    return (key_gradient, value_gradient)


def bucket_lookup(bucket, table):
    running = jnp.zeros((table.shape[1],) + bucket.shape, jnp.float32)
    for level in range(BUCKETS):
        running = jnp.where(bucket[None] == level, table[level][:, None, None], running)
    return running


def bucket_sums(bucket, logit_grads):
    totals = [
        jnp.sum(jnp.where(bucket[None] == level, logit_grads, 0.0), axis=(1, 2))
        for level in range(BUCKETS)
    ]
    return jnp.stack(totals, axis=0)


def pass_rim(rim, offset):
    return shifted(rim.astype(jnp.bfloat16), "ctx", offset).astype(rim.dtype)


def band_part(query_rows, key_rows, value_rows, grad_rows, clause_rows, table, score_scale):
    rows, width = query_rows.shape
    head_dim = width // HEADS
    wide = 2 * head_dim
    half = WINDOW // 2
    pair_rows = jnp.concatenate([key_rows[:, :wide], value_rows[:, :wide]], axis=1)
    extended, extended_clause = (
        with_halo(pair_rows, (("ctx", 0),), half),
        with_halo(clause_rows, (("ctx", 0),), half),
    )
    reach = rows + 2 * half
    nearby_key_rows = extended[:, :wide].reshape(reach, 2, head_dim)
    values_near = extended[:, wide:].reshape(reach, 2, head_dim)
    query_matrix = query_rows[:, :wide].reshape(rows, 2, head_dim)
    gradient_list = grad_rows[:, :wide].reshape(rows, 2, head_dim)
    start = lax.axis_index("ctx") * rows
    length = rows * lax.axis_size("ctx")
    local_query = jnp.arange(rows)[:, None]
    local_key = jnp.arange(reach)[None, :] - half
    global_key = start + local_key
    allowed = (jnp.abs(local_query - local_key) < half) & (global_key >= 0) & (global_key < length)
    bucket = jnp.minimum(jnp.abs(clause_rows[:, None] - extended_clause[None, :]), BUCKETS - 1)
    score_matrix = (
        jnp.einsum(
            "wvx,yvx->vwy", query_matrix, nearby_key_rows, preferred_element_type=jnp.float32
        )
        * score_scale
    )
    score_matrix = jnp.where(allowed[None], score_matrix + bucket_lookup(bucket, table), -jnp.inf)
    attended, query_gradient, softmax_weights, score_gradient, logit_grads, top, totals, delta = (
        rows_side(score_matrix, nearby_key_rows, values_near, gradient_list, score_scale)
    )
    key_gradient, value_gradient = keys_side(
        softmax_weights, score_gradient, query_matrix, gradient_list, score_scale
    )
    sums = jnp.concatenate(
        [key_gradient.reshape(reach, wide), value_gradient.reshape(reach, wide)], axis=1
    )
    own = sums[half : half + rows]
    from_next = pass_rim(sums[:half], -1)
    from_prev = pass_rim(sums[half + rows :], 1)
    own = own.at[rows - half :].add(from_next).at[:half].add(from_prev)
    own_key = own[:, :wide].reshape(rows, 2, head_dim)
    own_value = own[:, wide:].reshape(rows, 2, head_dim)
    return (attended, query_gradient, own_key, own_value, bucket_sums(bucket, logit_grads))


def dilated(
    query_rows, key_rows, value_rows, grad_rows, initial_flag, dilation_rate, bits, score_scale
):
    head_dim = query_rows.shape[1] // HEADS
    wide = 2 * head_dim
    picked_query = sample_rows(query_rows, initial_flag, dilation_rate)
    picked_key = sample_rows(key_rows, initial_flag, dilation_rate)
    picked_value = sample_rows(value_rows, initial_flag, dilation_rate)
    picked_grad = sample_rows(grad_rows, initial_flag, dilation_rate)
    count = picked_query.shape[0]
    gathered = span_rows(jnp.concatenate([picked_key, picked_value], axis=1), bits)
    gathered_rows = gathered.shape[0]
    every_key_rows = gathered[:, :wide].reshape(gathered_rows, 2, head_dim)
    every_value_rows = gathered[:, wide:].reshape(gathered_rows, 2, head_dim)
    query_matrix = picked_query.reshape(count, 2, head_dim)
    gradient_list = picked_grad.reshape(count, 2, head_dim)
    score_matrix = (
        jnp.einsum("wvx,yvx->vwy", query_matrix, every_key_rows, preferred_element_type=jnp.float32)
        * score_scale
    )
    attended, query_gradient, softmax_weights, score_gradient, logit_grads, top, totals, delta = (
        rows_side(score_matrix, every_key_rows, every_value_rows, gradient_list, score_scale)
    )
    key_gradient, value_gradient = keys_side(
        softmax_weights, score_gradient, query_matrix, gradient_list, score_scale
    )
    partial_sums = jnp.concatenate(
        [key_gradient.reshape(gathered_rows, wide), value_gradient.reshape(gathered_rows, wide)],
        axis=1,
    )
    own = span_sums(partial_sums, bits)
    own_key = own[:, :wide].reshape(count, 2, head_dim)
    own_value = own[:, wide:].reshape(count, 2, head_dim)
    return (
        spread_rows(attended, dilation_rate),
        spread_rows(query_gradient, dilation_rate),
        spread_rows(own_key, dilation_rate),
        spread_rows(own_value, dilation_rate),
    )


def shards(query, key, value, grad_out, clause, bias_table):
    query_rows = query[0]
    key_rows = key[0]
    value_rows = value[0]
    grad_rows = grad_out[0]
    clause_rows = clause[0]
    rows, width = query_rows.shape
    head_dim = width // HEADS
    score_scale = head_dim ** (-0.5)
    bucket_bit_count = lax.axis_size("ctx").bit_length() - 1
    band = band_part(
        query_rows, key_rows, value_rows, grad_rows, clause_rows, bias_table, score_scale
    )
    pieces = [band[:4]]
    for initial_flag, dilation_rate, bits in (
        (2, DILATION_FIRST, max(bucket_bit_count - 5, 1)),
        (4, DILATION_SECOND, bucket_bit_count - 2),
        (6, DILATION_THIRD, bucket_bit_count),
    ):
        pieces.append(
            dilated(
                query_rows,
                key_rows,
                value_rows,
                grad_rows,
                initial_flag,
                dilation_rate,
                bits,
                score_scale,
            )
        )
    bias_grad = lax.psum(band[4], ("dp", "ctx"))
    joined = [
        jnp.concatenate([piece[slot] for piece in pieces], axis=1)
        .reshape(1, rows, width)
        .astype(jnp.bfloat16)
        for slot in range(4)
    ]
    return (joined[0], joined[1], joined[2], joined[3], bias_grad)


def solution(mesh):
    in_specs = (
        P("dp", "ctx", None),
        P("dp", "ctx", None),
        P("dp", "ctx", None),
        P("dp", "ctx", None),
        P("dp", "ctx"),
        P(),
    )
    out_specs = (
        P("dp", "ctx", None),
        P("dp", "ctx", None),
        P("dp", "ctx", None),
        P("dp", "ctx", None),
        P(),
    )
    return jax.shard_map(shards, mesh=mesh, in_specs=in_specs, out_specs=out_specs, check_vma=False)
```

profile of v0, /device:TPU:0, one launch (start us, length us, event | category | flops | bytes accessed | tf_op | source)
XLA Modules:
  0.0 168.5 jit_solution(9156526535375958377)
XLA Ops:
  0.6 1.4 collective-permute-start.3
  2.1 6.0 %collective-permute-start.2 = (s32[256]{0:T(256)}, s32[256]{0:T(256)}, u32[]{:S(2)}, u32[]{:S(2)}) collective-permute-start(s32[256]{0:T(256)} %bitcast.424), channel_id=1, source_target_pairs={{0,1},{1,2},{2,3},{3,4},{4,5},{5,6},{6,7},{8,9},{9,10},{10,11},{11... | collective-permute-start | bytes 3080 | tf_op jit(solution)/shard_map/ppermute | solution.py:37
  11.6 5.7 %collective-permute-start = (bf16[256,512]{0,1:T(8,128)(2,1)}, bf16[256,512]{0,1:T(8,128)(2,1)}, u32[]{:S(2)}, u32[]{:S(2)}) collective-permute-start(bf16[256,512]{0,1:T(8,128)(2,1)} %pad_maximum_fusion.7), channel_id=1, source_target_pairs={{0,1},{1,2},{2,3},{3,4},{4,5},{5,6},{6,7},{8,9},{9,10},{10,11},{11... | collective-permute-start | bytes 786440 | tf_op jit(solution)/shard_map/ppermute | solution.py:37
  19.0 2.2 %collective-permute-start.6 = (bf16[8,512]{1,0:T(8,128)(2,1)}, bf16[8,512]{1,0:T(8,128)(2,1)}, u32[]{:S(2)}, u32[]{:S(2)}) collective-permute-start(bf16[8,512]{1,0:T(8,128)(2,1)} %pad_maximum_fusion.24), channel_id=1, source_target_pairs={{0,1},{1,0},{2,3},{3,2},{4,5},{5,4},{6,7},{7,6},{8,9},{9,8},{10,11... | collective-permute-start | bytes 24584 | tf_op jit(solution)/shard_map/ppermute | solution.py:21
  25.8 1.4 fusion.57
  30.8 2.0 %collective-permute-start.4 = (bf16[256,512]{0,1:T(8,128)(2,1)S(1)}, bf16[256,512]{0,1:T(8,128)(2,1)S(1)}, u32[]{:S(2)}, u32[]{:S(2)}) collective-permute-start(bf16[256,512]{0,1:T(8,128)(2,1)S(1)} %pad_maximum_fusion.8), channel_id=1, source_target_pairs={{0,1},{1,0},{2,3},{3,2},{4,5},{5,4},{6,7},{7,6},{8,9},{9,8},{10,11... | collective-permute-start | bytes 786440 | tf_op jit(solution)/shard_map/ppermute | solution.py:21
  34.2 1.6 collective-permute-start.7
  35.8 5.4 %fusion.55 = (pred[256,768]{0,1:T(8,128)(4,1)}, pred[256,768]{0,1:T(8,128)(4,1)S(1)}, pred[256,768]{0,1:T(8,128)(4,1)S(1)}, pred[256,768]{0,1:T(8,128)(4,1)S(1)}...) fusion(s32[768]{0:T(1024)S(1)} %pad_add_fusion, ...), kind=kLoop, calls=%fused_computation.117 | loop fusion | flops 6881280 | bytes 6295552 | tf_op jit(solution)/shard_map/eq | solution.py:141
  44.0 1.5 collective-permute-start.12
  51.3 2.8 %collective-permute-done.13 = bf16[32,512]{1,0:T(8,128)(2,1)S(1)} collective-permute-done((bf16[32,512]{1,0:T(8,128)(2,1)S(1)}, bf16[32,512]{1,0:T(8,128)(2,1)S(1)}, u32[]{:S(2)}, u32[]{:S(2)}) %collective-permute-start.13) | collective-permute-done | bytes 32800 | tf_op jit(solution)/shard_map/ppermute | solution.py:21
  54.5 3.3 %collective-permute-done.14 = bf16[16,512]{1,0:T(8,128)(2,1)S(1)} collective-permute-done((bf16[16,512]{1,0:T(8,128)(2,1)S(1)}, bf16[16,512]{1,0:T(8,128)(2,1)S(1)}, u32[]{:S(2)}, u32[]{:S(2)}) %collective-permute-start.14) | collective-permute-done | bytes 16416 | tf_op jit(solution)/shard_map/ppermute | solution.py:21
  60.0 1.7 collective-permute-done.15
  67.1 2.8 %convolution_bitcast_fusion = bf16[256,2,128]{0,2,1:T(8,128)(2,1)} fusion(bf16[512,2,128]{0,2,1:T(8,128)(2,1)} %bitcast.400, f32[2,256]{1,0:T(2,128)S(1)} %get-tuple-element.522, bf16[512,2,128]{0,2,1:T(8,128)(2,1)S(1)} %bitcast.368, bf16[256,1,128]{2,0,1:T(8,128)(2,1)S(1)} %bitcast.397, bf16[256,1,128]{2,0,1:T(8,128)(2,1)S(1)} %bitcast.393), kind=kOutput, calls=%fused_computation.55 | convolution fusion | flops 135332864 | bytes 788480 | tf_op jit(solution)/shard_map/ezb,beo->zeo/dot_general | solution.py:100
  70.5 1.4 pad_maximum_fusion.1
  73.1 6.9 %fusion.8 = f32[2,256,768]{1,2,0:T(8,128)S(1)} fusion(bf16[768,2,128]{0,2,1:T(8,128)(2,1)S(1)} %bitcast.355, bf16[256,2,128]{0,2,1:T(8,128)(2,1)} %bitcast.373, f32[2]{0:T(128)} %get-tuple-element.425, f32[2]{0:T(128)} %get-tuple-element.426, f32[2]{0:T(128)S(1)} %copy-done.98, f32[2]{0:T(128)S(1)} %copy-done.99, f32[2]{0:T(128)S(1)} %copy-done.100, ...), kind=kOutput, calls=%fused_computation.14 | convolution fusion | flops 114425856 | bytes 8585472 | tf_op jit(solution)/shard_map/wvx,yvx->vwy/dot_general | solution.py:180
  81.3 3.1 %fusion.14 = bf16[256,2,128]{0,2,1:T(8,128)(2,1)} fusion(bf16[768,2,128]{0,2,1:T(8,128)(2,1)S(1)} %bitcast.390, f32[2,256]{1,0:T(2,128)S(1)} %get-tuple-element.524, f32[2,256,768]{1,2,0:T(8,128)} %copy-done.6), kind=kOutput, calls=%fused_computation.59 | convolution fusion | flops 101909760 | bytes 2099200 | tf_op jit(solution)/shard_map/ezb,beo->zeo/dot_general | solution.py:100
  84.4 2.5 %fusion.65 = f32[2,768,128]{1,2,0:T(8,128)S(1)} fusion(bf16[256,2,128]{0,2,1:T(8,128)(2,1)} %bitcast.401, f32[2,256]{1,0:T(2,128)S(1)} %get-tuple-element.524, f32[2,256,768]{1,2,0:T(8,128)} %copy-done.6), kind=kOutput, calls=%fused_computation.137 | convolution fusion | flops 101844224 | bytes 2492416 | tf_op jit(solution)/shard_map/vjb,jvw->bvw/dot_general | solution.py:132
  87.0 1.6 fusion.6
  89.2 5.4 %select_reduce_fusion = (f32[2]{0:T(128)}, f32[2]{0:T(128)}, f32[2]{0:T(128)S(1)}, f32[2]{0:T(128)S(1)}, f32[2]{0:T(128)S(1)}, /*index=5*/f32[2]{0:T(128)S(1)}, ...) fusion(pred[256,768]{0,1:T(8,128)(4,1)S(1)} %copy-done.37, ...), kind=kLoop, calls=%fused_computation.15 | loop fusion | flops 15335388 | bytes 8261776 | tf_op jit(solution)/shard_map/reduce_sum | solution.py:147
  94.8 4.4 %select_reduce_fusion.18 = (f32[2]{0:T(128)}, f32[2]{0:T(128)}, f32[2]{0:T(128)}, f32[2]{0:T(128)}, f32[2]{0:T(128)}, /*index=5*/f32[2]{0:T(128)}, f32[2]{0:T(12...) fusion(f32[2,256,768]{1,2,0:T(8,128)S(1)} %get-tuple-element.42, ...), kind=kLoop, calls=%fused_computation.33 | loop fusion | flops 11010020 | bytes 4325488 | tf_op jit(solution)/shard_map/reduce_sum | solution.py:147
  105.2 2.0 %copy.403 = bf16[1,256,1024]{2,1,0:T(8,128)(2,1)} copy(bf16[1,256,1024]{1,2,0:T(8,128)(2,1)} %bitcast.351) | data formatting | bytes 1048576
  107.2 2.0 %copy.404 = bf16[1,256,1024]{2,1,0:T(8,128)(2,1)} copy(bf16[1,256,1024]{1,2,0:T(8,128)(2,1)} %bitcast.352) | data formatting | bytes 1048576
  118.7 4.6 %collective-permute-start.10 = (bf16[256,512]{0,1:T(8,128)(2,1)}, bf16[256,512]{0,1:T(8,128)(2,1)S(1)}, u32[]{:S(2)}, u32[]{:S(2)}) collective-permute-start(bf16[256,512]{0,1:T(8,128)(2,1)} %get-tuple-element.429), channel_id=1, source_target_pairs={{0,1},{1,2},{2,3},{3,4},{4,5},{5,6},{6,7},{8,9},{9,10},{10,11},{11... | collective-permute-start | bytes 786440 | tf_op jit(solution)/shard_map/ppermute | solution.py:27
  123.4 40.3 %psum.7 = f32[32,2]{0,1:T(2,128)} all-reduce(f32[32,2]{0,1:T(2,128)S(1)} %stack.131), channel_id=1, replica_groups=mesh['dp'=4,'ctx'=8] {'dp','ctx'}, use_global_device_ids=true, to_apply=%region_44.45 | all-reduce | flops 64 | bytes 512 | tf_op jit(solution)/shard_map/psum | solution.py:276
  (443 shorter events, 53.7 us)
Async XLA Ops:
  0.6 8.7 %copy-start = (bf16[1,256,1024]{2,1,0:T(8,128)(2,1)S(1)}, bf16[1,256,1024]{2,1,0:T(8,128)(2,1)}, u32[]{:S(2)}) copy-start(bf16[1,256,1024]{2,1,0:T(8,128)(2,1)} %param.64) | copy-start | bytes 1572868
  0.6 30.1 %collective-permute-start.3 = (s32[256]{0:T(256)}, s32[256]{0:T(256)}, u32[]{:S(2)}, u32[]{:S(2)}) collective-permute-start(s32[256]{0:T(256)} %bitcast.423), channel_id=1, source_target_pairs={{1,0},{2,1},{3,2},{4,3},{5,4},{6,5},{7,6},{9,8},{10,9},{11,10},{12... | collective-permute-start | bytes 3080 | tf_op jit(solution)/shard_map/ppermute | solution.py:38
  2.1 28.7 %collective-permute-start.2 = (s32[256]{0:T(256)}, s32[256]{0:T(256)}, u32[]{:S(2)}, u32[]{:S(2)}) collective-permute-start(s32[256]{0:T(256)} %bitcast.424), channel_id=1, source_target_pairs={{0,1},{1,2},{2,3},{3,4},{4,5},{5,6},{6,7},{8,9},{9,10},{10,11},{11... | collective-permute-start | bytes 3080 | tf_op jit(solution)/shard_map/ppermute | solution.py:37
  9.6 11.6 %copy-start.7 = (f32[32,2]{0,1:T(2,128)S(1)}, f32[32,2]{0,1:T(2,128)}, u32[]{:S(2)}) copy-start(f32[32,2]{0,1:T(2,128)} %param.67) | copy-start | bytes 772
  9.6 13.7 %copy-start.2 = (bf16[1,256,1024]{2,1,0:T(8,128)(2,1)S(1)}, bf16[1,256,1024]{2,1,0:T(8,128)(2,1)}, u32[]{:S(2)}) copy-start(bf16[1,256,1024]{2,1,0:T(8,128)(2,1)} %param.65) | copy-start | bytes 1572868
  10.4 60.1 %collective-permute-start.1 = (bf16[256,512]{0,1:T(8,128)(2,1)}, bf16[256,512]{0,1:T(8,128)(2,1)}, u32[]{:S(2)}, u32[]{:S(2)}) collective-permute-start(bf16[256,512]{0,1:T(8,128)(2,1)} %pad_maximum_fusion.7), channel_id=1, source_target_pairs={{1,0},{2,1},{3,2},{4,3},{5,4},{6,5},{7,6},{9,8},{10,9},{11,10},{12... | collective-permute-start | bytes 786440 | tf_op jit(solution)/shard_map/ppermute | solution.py:38
  11.6 58.8 %collective-permute-start = (bf16[256,512]{0,1:T(8,128)(2,1)}, bf16[256,512]{0,1:T(8,128)(2,1)}, u32[]{:S(2)}, u32[]{:S(2)}) collective-permute-start(bf16[256,512]{0,1:T(8,128)(2,1)} %pad_maximum_fusion.7), channel_id=1, source_target_pairs={{0,1},{1,2},{2,3},{3,4},{4,5},{5,6},{6,7},{8,9},{9,10},{10,11},{11... | collective-permute-start | bytes 786440 | tf_op jit(solution)/shard_map/ppermute | solution.py:37
  19.0 14.4 %collective-permute-start.6 = (bf16[8,512]{1,0:T(8,128)(2,1)}, bf16[8,512]{1,0:T(8,128)(2,1)}, u32[]{:S(2)}, u32[]{:S(2)}) collective-permute-start(bf16[8,512]{1,0:T(8,128)(2,1)} %pad_maximum_fusion.24), channel_id=1, source_target_pairs={{0,1},{1,0},{2,3},{3,2},{4,5},{5,4},{6,7},{7,6},{8,9},{9,8},{10,11... | collective-permute-start | bytes 24584 | tf_op jit(solution)/shard_map/ppermute | solution.py:21
  28.6 35.6 %copy-start.82 = (bf16[256,1,1,128]{3,0,2,1:T(8,128)(2,1)}, bf16[256,1,1,128]{3,0,2,1:T(8,128)(2,1)S(1)}, u32[]{:S(2)}) copy-start(bf16[256,1,1,128]{3,0,2,1:T(8,128)(2,1)S(1)} %copy.426) | copy-start | bytes 196612
  30.8 11.7 %collective-permute-start.5 = (bf16[32,512]{1,0:T(8,128)(2,1)S(1)}, bf16[32,512]{1,0:T(8,128)(2,1)S(1)}, u32[]{:S(2)}, u32[]{:S(2)}) collective-permute-start(bf16[32,512]{1,0:T(8,128)(2,1)S(1)} %pad_maximum_fusion.17), channel_id=1, source_target_pairs={{0,1},{1,0},{2,3},{3,2},{4,5},{5,4},{6,7},{7,6},{8,9},{9,8},{10,11... | collective-permute-start | bytes 98312 | tf_op jit(solution)/shard_map/ppermute | solution.py:21
  30.8 32.7 %collective-permute-start.4 = (bf16[256,512]{0,1:T(8,128)(2,1)S(1)}, bf16[256,512]{0,1:T(8,128)(2,1)S(1)}, u32[]{:S(2)}, u32[]{:S(2)}) collective-permute-start(bf16[256,512]{0,1:T(8,128)(2,1)S(1)} %pad_maximum_fusion.8), channel_id=1, source_target_pairs={{0,1},{1,0},{2,3},{3,2},{4,5},{5,4},{6,7},{7,6},{8,9},{9,8},{10,11... | collective-permute-start | bytes 786440 | tf_op jit(solution)/shard_map/ppermute | solution.py:21
  34.2 7.1 %collective-permute-start.7 = (bf16[16,512]{1,0:T(8,128)(2,1)S(1)}, bf16[16,512]{1,0:T(8,128)(2,1)S(1)}, u32[]{:S(2)}, u32[]{:S(2)}) collective-permute-start(bf16[16,512]{1,0:T(8,128)(2,1)S(1)} %maximum_select_fusion.4), channel_id=1, source_target_pairs={{0,2},{2,0},{1,3},{3,1},{4,6},{6,4},{5,7},{7,5},{8,10},{10,8},{9,1... | collective-permute-start | bytes 49160 | tf_op jit(solution)/shard_map/ppermute | solution.py:21
  41.3 31.4 %copy-start.8 = (pred[256,768]{0,1:T(8,128)(4,1)}, pred[256,768]{0,1:T(8,128)(4,1)S(1)}, u32[]{:S(2)}) copy-start(pred[256,768]{0,1:T(8,128)(4,1)S(1)} %get-tuple-element.487) | copy-start | bytes 589828
  41.3 31.4 %copy-start.10 = (pred[256,768]{0,1:T(8,128)(4,1)}, pred[256,768]{0,1:T(8,128)(4,1)S(1)}, u32[]{:S(2)}) copy-start(pred[256,768]{0,1:T(8,128)(4,1)S(1)} %get-tuple-element.488) | copy-start | bytes 589828
  41.3 31.4 %copy-start.12 = (pred[256,768]{0,1:T(8,128)(4,1)}, pred[256,768]{0,1:T(8,128)(4,1)S(1)}, u32[]{:S(2)}) copy-start(pred[256,768]{0,1:T(8,128)(4,1)S(1)} %get-tuple-element.489) | copy-start | bytes 589828
  41.3 6.0 %collective-permute-start.8 = (bf16[32,512]{1,0:T(8,128)(2,1)S(1)}, bf16[32,512]{1,0:T(8,128)(2,1)S(1)}, u32[]{:S(2)}, u32[]{:S(2)}) collective-permute-start(bf16[32,512]{1,0:T(8,128)(2,1)S(1)} %maximum_select_fusion.3), channel_id=1, source_target_pairs={{0,4},{4,0},{1,5},{5,1},{2,6},{6,2},{3,7},{7,3},{8,12},{12,8},{9,1... | collective-permute-start | bytes 98312 | tf_op jit(solution)/shard_map/ppermute | solution.py:21
  44.0 7.0 %collective-permute-start.12 = (bf16[32,512]{1,0:T(8,128)(2,1)S(1)}, bf16[32,512]{1,0:T(8,128)(2,1)S(1)}, u32[]{:S(2)}, u32[]{:S(2)}) collective-permute-start(bf16[32,512]{1,0:T(8,128)(2,1)S(1)} %select_convert_fusion.2), channel_id=1, source_target_pairs={{0,1},{1,0},{2,3},{3,2},{4,5},{5,4},{6,7},{7,6},{8,9},{9,8},{10,11... | collective-permute-start | bytes 98312 | tf_op jit(solution)/shard_map/ppermute | solution.py:21
  48.8 5.2 %collective-permute-start.13 = (bf16[32,512]{1,0:T(8,128)(2,1)S(1)}, bf16[32,512]{1,0:T(8,128)(2,1)S(1)}, u32[]{:S(2)}, u32[]{:S(2)}) collective-permute-start(bf16[32,512]{1,0:T(8,128)(2,1)S(1)} %select_convert_fusion.1), channel_id=1, source_target_pairs={{0,4},{4,0},{1,5},{5,1},{2,6},{6,2},{3,7},{7,3},{8,12},{12,8},{9,1... | collective-permute-start | bytes 98312 | tf_op jit(solution)/shard_map/ppermute | solution.py:21
  54.1 3.8 %collective-permute-start.14 = (bf16[16,512]{1,0:T(8,128)(2,1)S(1)}, bf16[16,512]{1,0:T(8,128)(2,1)S(1)}, u32[]{:S(2)}, u32[]{:S(2)}) collective-permute-start(bf16[16,512]{1,0:T(8,128)(2,1)S(1)} %select_convert_fusion.3), channel_id=1, source_target_pairs={{0,2},{2,0},{1,3},{3,1},{4,6},{6,4},{5,7},{7,5},{8,10},{10,8},{9,1... | collective-permute-start | bytes 49160 | tf_op jit(solution)/shard_map/ppermute | solution.py:21
  57.9 3.7 %collective-permute-start.15 = (bf16[8,512]{1,0:T(8,128)(2,1)S(1)}, bf16[8,512]{1,0:T(8,128)(2,1)S(1)}, u32[]{:S(2)}, u32[]{:S(2)}) collective-permute-start(bf16[8,512]{1,0:T(8,128)(2,1)S(1)} %select_convert_fusion.4), channel_id=1, source_target_pairs={{0,1},{1,0},{2,3},{3,2},{4,5},{5,4},{6,7},{7,6},{8,9},{9,8},{10,11... | collective-permute-start | bytes 24584 | tf_op jit(solution)/shard_map/ppermute | solution.py:21
  103.0 60.7 %collective-permute-start.11 = (bf16[256,512]{0,1:T(8,128)(2,1)}, bf16[256,512]{0,1:T(8,128)(2,1)}, u32[]{:S(2)}, u32[]{:S(2)}) collective-permute-start(bf16[256,512]{0,1:T(8,128)(2,1)} %select_convert_fusion), channel_id=1, source_target_pairs={{0,1},{1,0},{2,3},{3,2},{4,5},{5,4},{6,7},{7,6},{8,9},{9,8},{10,11... | collective-permute-start | bytes 786440 | tf_op jit(solution)/shard_map/ppermute | solution.py:21
  104.3 11.8 %copy-start.110 = (f32[2]{0:T(128)S(1)}, f32[2]{0:T(128)}, u32[]{:S(2)}) copy-start(f32[2]{0:T(128)} %get-tuple-element.390) | copy-start | bytes 28
  117.4 48.6 %collective-permute-start.9 = (bf16[256,512]{0,1:T(8,128)(2,1)}, bf16[256,512]{0,1:T(8,128)(2,1)S(1)}, u32[]{:S(2)}, u32[]{:S(2)}) collective-permute-start(bf16[256,512]{0,1:T(8,128)(2,1)} %get-tuple-element.428), channel_id=1, source_target_pairs={{1,0},{2,1},{3,2},{4,3},{5,4},{6,5},{7,6},{9,8},{10,9},{11,10},{12... | collective-permute-start | bytes 786440 | tf_op jit(solution)/shard_map/ppermute | solution.py:27
  118.7 47.4 %collective-permute-start.10 = (bf16[256,512]{0,1:T(8,128)(2,1)}, bf16[256,512]{0,1:T(8,128)(2,1)S(1)}, u32[]{:S(2)}, u32[]{:S(2)}) collective-permute-start(bf16[256,512]{0,1:T(8,128)(2,1)} %get-tuple-element.429), channel_id=1, source_target_pairs={{0,1},{1,2},{2,3},{3,4},{4,5},{5,6},{6,7},{8,9},{9,10},{10,11},{11... | collective-permute-start | bytes 786440 | tf_op jit(solution)/shard_map/ppermute | solution.py:27
  (107 other events, 349.1 us)
where the time goes:
time: 169 us; the launch traced here: 168 us
  blocking collectives  40.3 us (24%)
  local copies, waits for them, and re-layouts  37.5 us (22%)
  starting transfers between devices  30.3 us (18%)
  other arithmetic  26.3 us (16%)
  matrix products  23.4 us (14%)
  waiting for transfers between devices  7.82 us (5%)
  between operations  2.87 us (2%)
    psum x1, blocking collectives, shards(): bias_grad = lax.psum(band[4], ('dp', 'ctx'))  40.3 us
    unnamed x252, local copies, waits for them, and re-layouts  12.8 us
    ppermute x2, starting transfers between devices, with_halo(): before = lax.ppermute(last, axis, up)  11.7 us
    ppermute x10, starting transfers between devices, swapped(): return lax.ppermute(block, axis, route)  10.1 us
    reduce_sum x2, other arithmetic, bucket_sums(): jnp.sum(jnp.where(bucket[None] == level, logit_grads, 0.0), axis=(1, 2))  9.8 us
    ppermute x10, waiting for transfers between devices, swapped(): return lax.ppermute(block, axis, route)  7.8 us
    another operation x33, local copies, waits for them, and re-layouts, bucket_sums(): return jnp.stack(totals, axis=0)  7.42 us
    dot_general x1, matrix products, band_part(): jnp.einsum('wvx,yvx->vwy', query_matrix, nearby_key_rows, preferred_eleme...  6.9 us
  transfers between devices with their start and end apart: 16, of which 3 were waited for; matrix products, arithmetic and copies ran while one was open for 31% of the time, Pallas kernels for 0%

commit v1 on v0

--- a/solution.py
+++ b/solution.py
@@ -1,6 +1,8 @@
 import jax
 import jax.numpy as jnp
 from jax import lax
+from jax.experimental import pallas as pl
+from jax.experimental.pallas import tpu as pltpu
 from jax.sharding import PartitionSpec as P
 
 HEADS = 8
@@ -283,7 +285,7 @@
     return (joined[0], joined[1], joined[2], joined[3], bias_grad)
 
 
-def solution(mesh):
+def general(mesh):
     in_specs = (
         P("dp", "ctx", None),
         P("dp", "ctx", None),
@@ -300,3 +302,504 @@
         P(),
     )
     return jax.shard_map(shards, mesh=mesh, in_specs=in_specs, out_specs=out_specs, check_vma=False)
+
+
+ROWS = 256
+D = 128
+BF = jnp.bfloat16
+F32 = jnp.float32
+
+
+def mm(a, b, dims):
+    return lax.dot_general(a, b, (dims, ((), ())), preferred_element_type=F32)
+
+
+def nt(a, b):
+    return mm(a, b, ((1,), (1,)))
+
+
+def nn(a, b):
+    return mm(a, b, ((1,), (0,)))
+
+
+def tn(a, b):
+    return mm(a, b, ((0,), (0,)))
+
+
+def halves(x):
+    high = x.astype(BF)
+    return high, (x - high.astype(F32)).astype(BF)
+
+
+def softmax_grads(scores, q, k, v, g, scale):
+    top = jnp.max(scores, axis=-1, keepdims=True)
+    raised = jnp.exp(scores - top)
+    shares = raised * (1.0 / jnp.sum(raised, axis=-1, keepdims=True))
+    weights = shares.astype(BF)
+    attended = nn(weights, v)
+    weight_grads = nt(g, v)
+    delta = jnp.sum(shares * weight_grads, axis=-1, keepdims=True)
+    logit_grads = shares * (weight_grads - delta)
+    score_grads = logit_grads.astype(BF)
+    grad_q = nn(score_grads, k) * scale
+    grad_k = tn(score_grads, q) * scale
+    grad_v = tn(weights, g)
+    return attended, grad_q, grad_k, grad_v, logit_grads
+
+
+def selector(count, step, offset):
+    row = lax.broadcasted_iota(jnp.int32, (count, ROWS), 0)
+    col = lax.broadcasted_iota(jnp.int32, (count, ROWS), 1)
+    return (col == row * step + offset).astype(BF)
+
+
+def clause_column(row_form):
+    whole = row_form[...].astype(jnp.int32)
+    index = lax.broadcasted_iota(jnp.int32, whole.shape, 0)
+    parts = jnp.where(index == 0, whole >> 6, jnp.where(index == 1, whole & 63, 0))
+    line = lax.broadcasted_iota(jnp.int32, (8, D), 0)
+    factor = jnp.where(line == 0, 64.0, jnp.where(line == 1, 1.0, 0.0))
+    column = tn(parts.astype(F32).astype(BF), factor.astype(BF))
+    return column.astype(jnp.int32)
+
+
+def one_hot(column):
+    lane = lax.broadcasted_iota(jnp.int32, (ROWS, D), 1)
+    return (lane == (column & 127)).astype(F32).astype(BF)
+
+
+def main_kernel(
+    ctx_count, dp_count,
+    table_ref, clause_ref, q_ref, k_ref, v_ref, g_ref,
+    out_ref, second_ref, third_ref, bias_ref,
+    pair_buf, halo_buf, halo_clause, pair_clause, grad_buf, grad_send, ret_send, ret_buf,
+    s2, s3, bias_ctx, bias_dp,
+    send_sem, recv_sem, s3_send, s3_recv, bc_send, bc_recv, bd_send, bd_recv,
+):
+    me = lax.axis_index("ctx")
+    row = lax.axis_index("dp")
+    c = lax.rem(me, 2)
+    partner = me + 1 - 2 * c
+    outward = me - 2 + 4 * c
+    beyond = me + 2 - 4 * c
+    has_out = (outward >= 0) & (outward < ctx_count)
+    has_beyond = (beyond >= 0) & (beyond < ctx_count)
+    scale = D**-0.5
+    mesh_id = pl.DeviceIdType.MESH
+
+    barrier = pltpu.get_barrier_semaphore()
+    for step in range(1, ctx_count):
+        pl.semaphore_signal(
+            barrier, inc=1, device_id=(row, lax.rem(me + step, ctx_count)), device_id_type=mesh_id
+        )
+    for step in range(1, dp_count):
+        pl.semaphore_signal(
+            barrier, inc=1, device_id=(lax.rem(row + step, dp_count), me), device_id_type=mesh_id
+        )
+    pl.semaphore_wait(barrier, ctx_count + dp_count - 2)
+
+    def remote(src, dst, index, target):
+        return pltpu.make_async_remote_copy(
+            src_ref=src,
+            dst_ref=dst,
+            send_sem=send_sem.at[index],
+            recv_sem=recv_sem.at[index],
+            device_id=(row, target),
+            device_id_type=mesh_id,
+        )
+
+    def columns(head):
+        return pl.ds(pl.multiple_of(head * D, D), D)
+
+    inputs = (k_ref, v_ref, q_ref, g_ref)
+    band_out = [
+        remote(inputs[i].at[:, columns(1 - c)], pair_buf.at[i], i, partner) for i in range(4)
+    ]
+    first_out = [
+        remote(inputs[i].at[:, columns(3 - c)], pair_buf.at[4 + i], 4 + i, partner)
+        for i in range(4)
+    ]
+    clause_out = remote(clause_ref, pair_clause, 8, partner)
+    own_halo = [
+        remote(k_ref.at[:, columns(c)], halo_buf.at[1, 0], 9, outward),
+        remote(v_ref.at[:, columns(c)], halo_buf.at[1, 1], 10, outward),
+        remote(clause_ref, halo_clause.at[1], 11, outward),
+    ]
+    far_halo = [
+        remote(pair_buf.at[0], halo_buf.at[0, 0], 12, beyond),
+        remote(pair_buf.at[1], halo_buf.at[0, 1], 13, beyond),
+        remote(pair_clause, halo_clause.at[0], 14, beyond),
+    ]
+
+    clause_out.start()
+    for copy in band_out[:2]:
+        copy.start()
+
+    @pl.when(has_out)
+    def _():
+        for copy in own_halo:
+            copy.start()
+
+    for copy in band_out[2:]:
+        copy.start()
+    for copy in first_out:
+        copy.start()
+
+    for i, ref in enumerate((q_ref, k_ref, v_ref, g_ref)):
+        for h in range(2):
+            part = nn(selector(32, DILATION_SECOND, h * DILATION_SECOND // 2), ref[:, (4 + h) * D : (5 + h) * D])
+            s2[0, :, (2 * i + h) * D : (2 * i + h + 1) * D] = part.astype(BF)
+
+    def thirds(refs):
+        return jnp.concatenate(
+            [
+                nn(selector(8, DILATION_THIRD, h * DILATION_THIRD // 2), ref[:, (6 + h) * D : (7 + h) * D])
+                for ref in refs
+                for h in range(2)
+            ],
+            axis=1,
+        )
+
+    s3[0] = jnp.concatenate([thirds((q_ref, k_ref)), thirds((v_ref, g_ref))], axis=0).astype(BF)
+    second_out = remote(s2.at[0], s2.at[1], 15, partner)
+    second_out.start()
+    third_out = []
+    for step in range(1, ctx_count):
+        copy = pltpu.make_async_remote_copy(
+            src_ref=s3.at[0],
+            dst_ref=s3.at[ctx_count - step],
+            send_sem=s3_send.at[step],
+            recv_sem=s3_recv.at[ctx_count - step],
+            device_id=(row, lax.rem(me + step, ctx_count)),
+            device_id_type=mesh_id,
+        )
+        copy.start()
+        third_out.append(copy)
+
+    line = lax.broadcasted_iota(jnp.int32, (D, D), 0)
+    lane = lax.broadcasted_iota(jnp.int32, (D, D), 1)
+    apart = jnp.abs(((lane - line + 64) & 127) - 64)
+    table = jnp.zeros((D, D), F32)
+    for level in range(BUCKETS):
+        table = jnp.where(apart == level, table_ref[level, c], table)
+    far_bias = table_ref[BUCKETS - 1, c]
+    table_high, table_low = halves(table)
+
+    clause_out.wait_recv()
+    band_out[0].wait_recv()
+    band_out[1].wait_recv()
+
+    @pl.when(has_beyond)
+    def _():
+        for copy in far_halo:
+            copy.start()
+
+    @pl.when(jnp.logical_not(has_out))
+    def _():
+        halo_buf[0] = jnp.zeros((2, ROWS, D), BF)
+        halo_clause[0] = jnp.zeros((8, ROWS), jnp.int32)
+
+    @pl.when(jnp.logical_not(has_beyond))
+    def _():
+        halo_buf[1] = jnp.zeros((2, ROWS, D), BF)
+        halo_clause[1] = jnp.zeros((8, ROWS), jnp.int32)
+
+    band_out[2].wait_recv()
+    band_out[3].wait_recv()
+
+    own = [ref[:, columns(c)] for ref in inputs]
+    other = [pair_buf[i] for i in range(4)]
+    clauses = {"own": clause_ref, "other": pair_clause}
+    cols = {name: clause_column(ref) for name, ref in clauses.items()}
+    hots = {name: one_hot(col) for name, col in cols.items()}
+    line = lax.broadcasted_iota(jnp.int32, (ROWS, ROWS), 0)
+    lane = lax.broadcasted_iota(jnp.int32, (ROWS, ROWS), 1)
+    diff = (line - lane) * (1 - 2 * c)
+
+    def band_block(slot, mine, near, mine_name, near_name, sign, halo_valid):
+        k = jnp.concatenate([mine[0], near[0], halo_buf[slot, 0]], axis=0)
+        v = jnp.concatenate([mine[1], near[1], halo_buf[slot, 1]], axis=0)
+        q, g = mine[2], mine[3]
+        halo_hot = one_hot(clause_column(halo_clause.at[slot]))
+        key_hot = jnp.concatenate([hots[mine_name], hots[near_name], halo_hot], axis=0)
+        key_row = jnp.concatenate(
+            [clauses[mine_name][0:1, :], clauses[near_name][0:1, :], halo_clause[slot, 0:1, :]],
+            axis=1,
+        )
+        query_hot = hots[mine_name]
+        close = jnp.abs(cols[mine_name][:, 0:1] - key_row) < BUCKETS - 1
+        spread = jnp.concatenate(
+            [nn(query_hot, table_high).astype(BF), nn(query_hot, table_low).astype(BF)], axis=1
+        )
+        bias = nt(spread, jnp.concatenate([key_hot, key_hot], axis=1))
+        signed = diff * sign
+        reach = jnp.where(halo_valid, 0, ROWS)
+        allowed = jnp.concatenate(
+            [jnp.ones((ROWS, ROWS), jnp.int32), jnp.where(signed > 0, 1, 0), jnp.where(-signed > reach, 1, 0)],
+            axis=1,
+        )
+        scores = nt(q, k) * scale + jnp.where(close, bias, far_bias)
+        scores = jnp.where(allowed > 0, scores, -jnp.inf)
+        attended, grad_q, grad_k, grad_v, logit_grads = softmax_grads(scores, q, k, v, g, scale)
+        kept = jnp.where(close, logit_grads, 0.0)
+        rest = jnp.sum(jnp.where(close, 0.0, logit_grads), axis=0, keepdims=True)
+        high, low = halves(kept)
+        by_clause = nn(high, key_hot) + nn(low, key_hot)
+        high, low = halves(by_clause)
+        pairs = tn(query_hot, high) + tn(query_hot, low) + tn(high, query_hot) + tn(low, query_hot)
+        return attended, grad_q, grad_k, grad_v, pairs, rest
+
+    @pl.when(has_out)
+    def _():
+        for copy in far_halo:
+            copy.wait_recv()
+
+    attended, grad_q, gk_a, gv_a, pairs_a, rest_a = band_block(
+        0, own, other, "own", "other", 1, has_out
+    )
+    out_ref[0, c] = attended.astype(BF)
+    out_ref[1, c] = grad_q.astype(BF)
+    grad_send[0, 0] = gk_a[2 * ROWS :].astype(BF)
+    grad_send[0, 1] = gv_a[2 * ROWS :].astype(BF)
+    back_out = remote(grad_send.at[0], grad_buf.at[0], 16, outward)
+    back_far = remote(grad_send.at[1], grad_buf.at[1], 17, beyond)
+
+    @pl.when(has_out)
+    def _():
+        back_out.start()
+
+    @pl.when(has_beyond)
+    def _():
+        for copy in own_halo:
+            copy.wait_recv()
+
+    attended, grad_q, gk_b, gv_b, pairs_b, rest_b = band_block(
+        1, other, own, "other", "own", -1, has_beyond
+    )
+    ret = [remote(ret_send.at[i], ret_buf.at[i], 18 + i, partner) for i in range(8)]
+    ret_send[0] = attended.astype(BF)
+    ret_send[1] = grad_q.astype(BF)
+    grad_send[1, 0] = gk_b[2 * ROWS :].astype(BF)
+    grad_send[1, 1] = gv_b[2 * ROWS :].astype(BF)
+
+    @pl.when(has_beyond)
+    def _():
+        back_far.start()
+
+    ret[0].start()
+    ret[1].start()
+    own_gk = gk_a[:ROWS] + gk_b[ROWS : 2 * ROWS]
+    own_gv = gv_a[:ROWS] + gv_b[ROWS : 2 * ROWS]
+    other_gk = gk_b[:ROWS] + gk_a[ROWS : 2 * ROWS]
+    other_gv = gv_b[:ROWS] + gv_a[ROWS : 2 * ROWS]
+
+    turned = pairs_a + pairs_b
+    line = lax.broadcasted_iota(jnp.int32, (D, D), 0)
+    for bit in range(7):
+        shift = 1 << bit
+        rolled = jnp.concatenate([turned[:, shift:], turned[:, :shift]], axis=1)
+        turned = jnp.where((line & shift) > 0, rolled, turned)
+    sums = jnp.sum(turned, axis=0, keepdims=True)
+    rest = jnp.sum(rest_a + rest_b, axis=1, keepdims=True)
+    lane = lax.broadcasted_iota(jnp.int32, (1, D), 1)
+    sums = jnp.where(lane == 0, 0.5 * sums, sums)
+    sums = jnp.where(lane < BUCKETS - 1, sums, jnp.where(lane == BUCKETS - 1, rest, 0.0))
+    tile_line = lax.broadcasted_iota(jnp.int32, (8, D), 0)
+    bias_ctx[me] = jnp.where(tile_line == c, sums, 0.0)
+    bias_out = []
+    for step in range(1, ctx_count):
+        copy = pltpu.make_async_remote_copy(
+            src_ref=bias_ctx.at[me],
+            dst_ref=bias_ctx.at[me],
+            send_sem=bc_send.at[step],
+            recv_sem=bc_recv.at[step],
+            device_id=(row, lax.rem(me + step, ctx_count)),
+            device_id_type=mesh_id,
+        )
+        copy.start()
+        bias_out.append(copy)
+
+    for copy in first_out:
+        copy.wait_recv()
+    k, v, q, g = [
+        jnp.concatenate([inputs[i][:, columns(2 + c)], pair_buf[4 + i]], axis=0) for i in range(4)
+    ]
+    results = softmax_grads(nt(q, k) * scale, q, k, v, g, scale)[:4]
+    for i in range(4):
+        out_ref[4 + i, c] = results[i][:ROWS].astype(BF)
+        ret_send[4 + i] = results[i][ROWS:].astype(BF)
+        ret[4 + i].start()
+
+    @pl.when(has_beyond)
+    def _():
+        back_out.wait_recv()
+
+    @pl.when(has_out)
+    def _():
+        back_far.wait_recv()
+
+    from_beyond = jnp.where(has_beyond, 1.0, 0.0)
+    from_out = jnp.where(has_out, 1.0, 0.0)
+
+    @pl.when(jnp.logical_not(has_beyond))
+    def _():
+        grad_buf[0] = jnp.zeros((2, ROWS, D), BF)
+
+    @pl.when(jnp.logical_not(has_out))
+    def _():
+        grad_buf[1] = jnp.zeros((2, ROWS, D), BF)
+
+    ret_send[2] = (other_gk + grad_buf[0, 0].astype(F32)).astype(BF)
+    ret_send[3] = (other_gv + grad_buf[0, 1].astype(F32)).astype(BF)
+    ret[2].start()
+    ret[3].start()
+    out_ref[2, c] = (own_gk + grad_buf[1, 0].astype(F32)).astype(BF)
+    out_ref[3, c] = (own_gv + grad_buf[1, 1].astype(F32)).astype(BF)
+
+    for copy in bias_out:
+        copy.wait_recv()
+    total = bias_ctx[0]
+    for i in range(1, ctx_count):
+        total = total + bias_ctx[i]
+    bias_dp[row] = total
+    docs_out = []
+    for step in range(1, dp_count):
+        copy = pltpu.make_async_remote_copy(
+            src_ref=bias_dp.at[row],
+            dst_ref=bias_dp.at[row],
+            send_sem=bd_send.at[step],
+            recv_sem=bd_recv.at[step],
+            device_id=(lax.rem(row + step, dp_count), me),
+            device_id_type=mesh_id,
+        )
+        copy.start()
+        docs_out.append(copy)
+
+    second_out.wait_recv()
+    both = jnp.concatenate([s2[0], s2[1]], axis=0)
+    for h in range(2):
+        q, k, v, g = [both[:, (2 * i + h) * D : (2 * i + h + 1) * D] for i in range(4)]
+        results = softmax_grads(nt(q, k) * scale, q, k, v, g, scale)[:4]
+        for i in range(4):
+            second_ref[i, :, h * D : (h + 1) * D] = results[i][:32]
+
+    for copy in third_out:
+        copy.wait_recv()
+    blocks = [s3[i].astype(F32) for i in range(ctx_count)]
+    upper = jnp.concatenate([block[:8] for block in blocks], axis=0).astype(BF)
+    lower = jnp.concatenate([block[8:] for block in blocks], axis=0).astype(BF)
+    for h in range(2):
+        q, k = [upper[:, (2 * i + h) * D : (2 * i + h + 1) * D] for i in range(2)]
+        v, g = [lower[:, (2 * i + h) * D : (2 * i + h + 1) * D] for i in range(2)]
+        results = softmax_grads(nt(q, k) * scale, q, k, v, g, scale)[:4]
+        for i in range(4):
+            third_ref[i, :, h * D : (h + 1) * D] = results[i][:8]
+
+    for copy in docs_out:
+        copy.wait_recv()
+    total = bias_dp[0]
+    for i in range(1, dp_count):
+        total = total + bias_dp[i]
+    bias_ref[...] = total
+
+    for i in (4, 5, 6, 7, 0, 1, 2, 3):
+        ret[i].wait_recv()
+        out_ref[i, 1 - c] = ret_buf[i]
+
+    for copy in band_out + first_out + [clause_out, second_out] + third_out + bias_out + docs_out + ret:
+        copy.wait_send()
+
+    @pl.when(has_out)
+    def _():
+        for copy in own_halo + [back_out]:
+            copy.wait_send()
+
+    @pl.when(has_beyond)
+    def _():
+        for copy in far_halo + [back_far]:
+            copy.wait_send()
+
+
+def layout_kernel(heads_ref, second_ref, third_ref, *outs):
+    for i, out in enumerate(outs):
+        for h in range(2):
+            out[:, h * D : (h + 1) * D] = heads_ref[i, h]
+            out[:, (2 + h) * D : (3 + h) * D] = heads_ref[4 + i, h]
+            seconds = second_ref[i, :, h * D : (h + 1) * D].astype(BF)
+            spread = tn(selector(32, DILATION_SECOND, h * DILATION_SECOND // 2), seconds)
+            out[:, (4 + h) * D : (5 + h) * D] = spread.astype(BF)
+            thirds = third_ref[i, :, h * D : (h + 1) * D].astype(BF)
+            spread = tn(selector(8, DILATION_THIRD, h * DILATION_THIRD // 2), thirds)
+            out[:, (6 + h) * D : (7 + h) * D] = spread.astype(BF)
+
+
+def paired(ctx_count, dp_count, query, key, value, grad_out, clause, bias_table):
+    vmem = pl.BlockSpec(memory_space=pltpu.VMEM)
+    smem = pl.BlockSpec(memory_space=pltpu.SMEM)
+    rows = jnp.broadcast_to(clause, (8, ROWS))
+    dma = pltpu.SemaphoreType.DMA
+    block = (ROWS, D)
+    heads, second, third, bias = pl.pallas_call(
+        lambda *refs: main_kernel(ctx_count, dp_count, *refs),
+        out_shape=[
+            jax.ShapeDtypeStruct((8, 2) + block, BF),
+            jax.ShapeDtypeStruct((4, 32, 2 * D), F32),
+            jax.ShapeDtypeStruct((4, 8, 2 * D), F32),
+            jax.ShapeDtypeStruct((8, D), F32),
+        ],
+        in_specs=[smem] + [vmem] * 5,
+        out_specs=[vmem] * 4,
+        scratch_shapes=[
+            pltpu.VMEM((8,) + block, BF),
+            pltpu.VMEM((2, 2) + block, BF),
+            pltpu.VMEM((2, 8, ROWS), jnp.int32),
+            pltpu.VMEM((8, ROWS), jnp.int32),
+            pltpu.VMEM((2, 2) + block, BF),
+            pltpu.VMEM((2, 2) + block, BF),
+            pltpu.VMEM((8,) + block, BF),
+            pltpu.VMEM((8,) + block, BF),
+            pltpu.VMEM((2, 32, 8 * D), BF),
+            pltpu.VMEM((ctx_count, 16, 4 * D), BF),
+            pltpu.VMEM((ctx_count, 8, D), F32),
+            pltpu.VMEM((dp_count, 8, D), F32),
+            dma((26,)),
+            dma((26,)),
+            dma((ctx_count,)),
+            dma((ctx_count,)),
+            dma((ctx_count,)),
+            dma((ctx_count,)),
+            dma((dp_count,)),
+            dma((dp_count,)),
+        ],
+        compiler_params=pltpu.CompilerParams(
+            collective_id=0, has_side_effects=True, vmem_limit_bytes=48 * 1024 * 1024
+        ),
+        name="attend",
+    )(bias_table, rows, query[0], key[0], value[0], grad_out[0])
+    outs = pl.pallas_call(
+        layout_kernel,
+        out_shape=[jax.ShapeDtypeStruct((ROWS, HEADS * D), BF)] * 4,
+        in_specs=[vmem] * 3,
+        out_specs=[vmem] * 4,
+        compiler_params=pltpu.CompilerParams(vmem_limit_bytes=32 * 1024 * 1024),
+        name="layout",
+    )(heads, second, third)
+    return tuple(out[None] for out in outs) + (bias[:2, :BUCKETS].T,)
+
+
+def solution(mesh):
+    ctx_count, dp_count = mesh.shape["ctx"], mesh.shape["dp"]
+    if ctx_count != 8:
+        return general(mesh)
+    spec = P("dp", "ctx", None)
+
+    def body(*arrays):
+        return paired(ctx_count, dp_count, *arrays)
+
+    return jax.shard_map(
+        body,
+        mesh=mesh,
+        in_specs=(spec, spec, spec, spec, P("dp", "ctx"), P()),
+        out_specs=(spec, spec, spec, spec, P()),
+        check_vma=False,
+    )

time: 169 us -> 43.4 us (0.26)
  blocking collectives: 40.3 us -> 0 us
  Pallas kernels: 0 us -> 36.3 us
  local copies, waits for them, and re-layouts: 37.5 us -> 6.17 us
  starting transfers between devices: 30.3 us -> 0 us
  other arithmetic: 26.3 us -> 0 us
  matrix products: 23.4 us -> 0 us
  waiting for transfers between devices: 7.82 us -> 0 us
  between operations: 2.87 us -> 0.65 us
    psum x1 -> x0, blocking collectives: 40.3 us -> none  [shards(): bias_grad = lax.psum(band[4], ('dp', 'ctx'))]
    pallas_call x0 -> x2, Pallas kernels: none -> 36.3 us  [the longest x1 34.5 us: paired(): pl.pallas_call(lambda *refs: main_kernel(ctx_count, dp_count, *refs), out...]
    ppermute x16 -> x0, starting transfers between devices: 30.3 us -> none  [the longest x2 11.7 us: with_halo(): before = lax.ppermute(last, axis, up)]
    dot_general x21 -> x0, matrix products: 22.3 us -> none  [the longest x1 6.9 us: band_part(): jnp.einsum('wvx,yvx->vwy', query_matrix, nearby_key_rows, preferred_eleme...]
    reduce_sum x2 -> x0, other arithmetic: 9.8 us -> none  [bucket_sums(): jnp.sum(jnp.where(bucket[None] == level, logit_grads, 0.0), axis=(1, 2))]
    another operation x53 -> x0, local copies, waits for them, and re-layouts: 8.84 us -> none  [the longest x33 7.42 us: bucket_sums(): return jnp.stack(totals, axis=0)]
    ppermute x16 -> x0, waiting for transfers between devices: 7.82 us -> none  [the longest x10 7.8 us: swapped(): return lax.ppermute(block, axis, route)]
    unnamed x252 -> x13, local copies, waits for them, and re-layouts: 12.8 us -> 5.6 us
  transfers between devices with their start and end apart: 16 -> 0, of which waited for: 3 -> 0; matrix products, arithmetic and copies ran while one was open for 31% -> 0% of each run, Pallas kernels for 0% -> 0%
where the time goes in v1:
time: 43.4 us; the launch traced here: 43.1 us
  Pallas kernels  36.3 us (84%)
  local copies, waits for them, and re-layouts  6.17 us (14%)
  between operations  0.65 us (1%)
    pallas_call x1, Pallas kernels, paired(): pl.pallas_call(lambda *refs: main_kernel(ctx_count, dp_count, *refs), out...  34.5 us
    unnamed x13, local copies, waits for them, and re-layouts  5.6 us
    pallas_call x1, Pallas kernels, paired(): pl.pallas_call(layout_kernel, out_shape=[jax.ShapeDtypeStruct((ROWS, HEAD...  1.78 us

profile of v1, /device:TPU:0, one launch (start us, length us, event | category | flops | bytes accessed | tf_op | source)
XLA Modules:
  0.0 43.1 jit_solution(9219930762018894308)
XLA Ops:
  0.6 0.0 copy-start.4
  0.6 0.7 %copy-done.4 = s32[1,256]{1,0:T(1,128)S(1)} copy-done((s32[1,256]{1,0:T(1,128)S(1)}, s32[1,256]{1,0:T(1,128)}, u32[]{:S(2)}) %copy-start.4) | copy-done | bytes 1048
  1.3 0.0 copy-start.5
  1.3 0.7 %copy-done.5 = f32[32,2]{0,1:T(2,128)S(1)} copy-done((f32[32,2]{0,1:T(2,128)S(1)}, f32[32,2]{0,1:T(2,128)}, u32[]{:S(2)}) %copy-start.5) | copy-done | bytes 280
  2.0 0.1 copy.11.refs_0_
  2.1 0.0 copy-start
  2.1 1.0 %copy-done = bf16[1,256,1024]{2,1,0:T(8,128)(2,1)S(1)} copy-done((bf16[1,256,1024]{2,1,0:T(8,128)(2,1)S(1)}, bf16[1,256,1024]{2,1,0:T(8,128)(2,1)}, u32[]{:S(2)}) %copy-start) | copy-done | bytes 524312
  3.1 0.0 copy-start.1
  3.1 1.0 %copy-done.1 = bf16[1,256,1024]{2,1,0:T(8,128)(2,1)S(1)} copy-done((bf16[1,256,1024]{2,1,0:T(8,128)(2,1)S(1)}, bf16[1,256,1024]{2,1,0:T(8,128)(2,1)}, u32[]{:S(2)}) %copy-start.1) | copy-done | bytes 524312
  4.2 0.0 copy-start.2
  4.2 1.0 %copy-done.2 = bf16[1,256,1024]{2,1,0:T(8,128)(2,1)S(1)} copy-done((bf16[1,256,1024]{2,1,0:T(8,128)(2,1)S(1)}, bf16[1,256,1024]{2,1,0:T(8,128)(2,1)}, u32[]{:S(2)}) %copy-start.2) | copy-done | bytes 524312
  5.2 0.0 copy-start.3
  5.2 1.0 %copy-done.3 = bf16[1,256,1024]{2,1,0:T(8,128)(2,1)S(1)} copy-done((bf16[1,256,1024]{2,1,0:T(8,128)(2,1)S(1)}, bf16[1,256,1024]{2,1,0:T(8,128)(2,1)}, u32[]{:S(2)}) %copy-start.3) | copy-done | bytes 524312
  6.2 34.5 %attend.1 = (bf16[8,2,256,128]{3,2,1,0:T(8,128)(2,1)S(1)}, f32[4,32,256]{2,1,0:T(8,128)S(1)}, f32[4,8,256]{2,1,0:T(8,128)S(1)}, f32[8,128]{1,0:T(8,128)S(1)}) custom-call(f32[32,2]{1,0:T(8,128)S(1)} %copy.11.refs_0_, s32[8,256]{1,0:T(8,128)S(1)} %broadcast_in_dim.20.refs_1_, bf16[256,1024]{1,0:T(8,128)(2,1)S(1)} %bitcast.11, bf16[256,1024]{1,0:T(8,128)(2,1)S(1)} %bitcast.12, ...), custom_call_target="tpu_custom_call" | custom-call | tf_op jit(solution)/shard_map/attend/pallas_call | solution.py:742
  40.8 0.6 %slice_bitcast_fusion = f32[32,2]{0,1:T(2,128)} fusion(f32[8,128]{1,0:T(8,128)S(1)} %get-tuple-element.20), kind=kLoop, calls=%fused_computation | loop fusion | bytes 512 | tf_op jit(solution)/shard_map/transpose | solution.py:787
  41.3 1.8 %layout.1 = (bf16[256,1024]{1,0:T(8,128)(2,1)}, bf16[256,1024]{1,0:T(8,128)(2,1)}, bf16[256,1024]{1,0:T(8,128)(2,1)}, bf16[256,1024]{1,0:T(8,128)(2,1)}) custom-call(bf16[8,2,256,128]{3,2,1,0:T(8,128)(2,1)S(1)} %get-tuple-element.13.heads_ref, f32[4,32,256]{2,1,0:T(8,128)S(1)} %get-tuple-element.14.second_ref, f32[4,8,256]{2,1,0:T(8,128)S(1)} %get-tuple-element.15.third_ref), custom_call_target="tpu_custom_call" | custom-call | tf_op jit(solution)/shard_map/layout/pallas_call | solution.py:779
  (1 shorter events, 0.0 us)
Async XLA Ops:
  0.6 0.7 %copy-start.4 = (s32[1,256]{1,0:T(1,128)S(1)}, s32[1,256]{1,0:T(1,128)}, u32[]{:S(2)}) copy-start(s32[1,256]{1,0:T(1,128)} %param.10) | copy-start | bytes 3076
  1.3 0.7 %copy-start.5 = (f32[32,2]{0,1:T(2,128)S(1)}, f32[32,2]{0,1:T(2,128)}, u32[]{:S(2)}) copy-start(f32[32,2]{0,1:T(2,128)} %param.11) | copy-start | bytes 772
  2.1 1.0 %copy-start = (bf16[1,256,1024]{2,1,0:T(8,128)(2,1)S(1)}, bf16[1,256,1024]{2,1,0:T(8,128)(2,1)}, u32[]{:S(2)}) copy-start(bf16[1,256,1024]{2,1,0:T(8,128)(2,1)} %param.6) | copy-start | bytes 1572868
  3.1 1.0 %copy-start.1 = (bf16[1,256,1024]{2,1,0:T(8,128)(2,1)S(1)}, bf16[1,256,1024]{2,1,0:T(8,128)(2,1)}, u32[]{:S(2)}) copy-start(bf16[1,256,1024]{2,1,0:T(8,128)(2,1)} %param.7) | copy-start | bytes 1572868
  4.2 1.0 %copy-start.2 = (bf16[1,256,1024]{2,1,0:T(8,128)(2,1)S(1)}, bf16[1,256,1024]{2,1,0:T(8,128)(2,1)}, u32[]{:S(2)}) copy-start(bf16[1,256,1024]{2,1,0:T(8,128)(2,1)} %param.8) | copy-start | bytes 1572868
  5.2 1.0 %copy-start.3 = (bf16[1,256,1024]{2,1,0:T(8,128)(2,1)S(1)}, bf16[1,256,1024]{2,1,0:T(8,128)(2,1)}, u32[]{:S(2)}) copy-start(bf16[1,256,1024]{2,1,0:T(8,128)(2,1)} %param.9) | copy-start | bytes 1572868

commit v2 on v1

--- a/solution.py
+++ b/solution.py
@@ -354,7 +354,7 @@
 
 
 def clause_column(row_form):
-    whole = row_form[...].astype(jnp.int32)
+    whole = jnp.broadcast_to(row_form[...], (8, ROWS))
     index = lax.broadcasted_iota(jnp.int32, whole.shape, 0)
     parts = jnp.where(index == 0, whole >> 6, jnp.where(index == 1, whole & 63, 0))
     line = lax.broadcasted_iota(jnp.int32, (8, D), 0)
@@ -370,9 +370,10 @@
 
 def main_kernel(
     ctx_count, dp_count,
-    table_ref, clause_ref, q_ref, k_ref, v_ref, g_ref,
+    table_hbm, clause_hbm, q_ref, k_ref, v_ref, g_ref,
     out_ref, second_ref, third_ref, bias_ref,
-    pair_buf, halo_buf, halo_clause, pair_clause, grad_buf, grad_send, ret_send, ret_buf,
+    table_ref, clause_ref, local, sampled, mine_send, local_sem, out_sem,
+    pair_buf, halo_buf, halo_clause, pair_clause, grad_buf, grad_send, ret_send,
     s2, s3, bias_ctx, bias_dp,
     send_sem, recv_sem, s3_send, s3_recv, bc_send, bc_recv, bd_send, bd_recv,
 ):
@@ -387,6 +388,26 @@
     scale = D**-0.5
     mesh_id = pl.DeviceIdType.MESH
 
+    def columns(head):
+        return pl.ds(pl.multiple_of(head * D, D), D)
+
+    inputs = (k_ref, v_ref, q_ref, g_ref)
+    loads = [
+        pltpu.make_async_copy(ref.at[:, columns(2 * j + c)], local.at[i, j], local_sem.at[2 * i + j])
+        for i, ref in enumerate(inputs)
+        for j in range(2)
+    ]
+    sample_loads = [
+        pltpu.make_async_copy(ref.at[:, 4 * D :], sampled.at[i], local_sem.at[8 + i])
+        for i, ref in enumerate(inputs)
+    ]
+    small_loads = [
+        pltpu.make_async_copy(clause_hbm, clause_ref, local_sem.at[12]),
+        pltpu.make_async_copy(table_hbm, table_ref, local_sem.at[13]),
+    ]
+    for copy in sample_loads + small_loads + loads:
+        copy.start()
+
     barrier = pltpu.get_barrier_semaphore()
     for step in range(1, ctx_count):
         pl.semaphore_signal(
@@ -408,10 +429,6 @@
             device_id_type=mesh_id,
         )
 
-    def columns(head):
-        return pl.ds(pl.multiple_of(head * D, D), D)
-
-    inputs = (k_ref, v_ref, q_ref, g_ref)
     band_out = [
         remote(inputs[i].at[:, columns(1 - c)], pair_buf.at[i], i, partner) for i in range(4)
     ]
@@ -419,11 +436,11 @@
         remote(inputs[i].at[:, columns(3 - c)], pair_buf.at[4 + i], 4 + i, partner)
         for i in range(4)
     ]
-    clause_out = remote(clause_ref, pair_clause, 8, partner)
+    clause_out = remote(clause_hbm, pair_clause, 8, partner)
     own_halo = [
         remote(k_ref.at[:, columns(c)], halo_buf.at[1, 0], 9, outward),
         remote(v_ref.at[:, columns(c)], halo_buf.at[1, 1], 10, outward),
-        remote(clause_ref, halo_clause.at[1], 11, outward),
+        remote(clause_hbm, halo_clause.at[1], 11, outward),
     ]
     far_halo = [
         remote(pair_buf.at[0], halo_buf.at[0, 0], 12, beyond),
@@ -440,27 +457,24 @@
         for copy in own_halo:
             copy.start()
 
-    for copy in band_out[2:]:
-        copy.start()
-    for copy in first_out:
-        copy.start()
-
-    for i, ref in enumerate((q_ref, k_ref, v_ref, g_ref)):
+    for copy in sample_loads:
+        copy.wait()
+    for i, ref in enumerate((sampled.at[2], sampled.at[0], sampled.at[1], sampled.at[3])):
         for h in range(2):
-            part = nn(selector(32, DILATION_SECOND, h * DILATION_SECOND // 2), ref[:, (4 + h) * D : (5 + h) * D])
+            part = nn(selector(32, DILATION_SECOND, h * DILATION_SECOND // 2), ref[:, h * D : (h + 1) * D])
             s2[0, :, (2 * i + h) * D : (2 * i + h + 1) * D] = part.astype(BF)
 
     def thirds(refs):
         return jnp.concatenate(
             [
-                nn(selector(8, DILATION_THIRD, h * DILATION_THIRD // 2), ref[:, (6 + h) * D : (7 + h) * D])
+                nn(selector(8, DILATION_THIRD, h * DILATION_THIRD // 2), ref[:, (2 + h) * D : (3 + h) * D])
                 for ref in refs
                 for h in range(2)
             ],
             axis=1,
         )
 
-    s3[0] = jnp.concatenate([thirds((q_ref, k_ref)), thirds((v_ref, g_ref))], axis=0).astype(BF)
+    s3[0] = jnp.concatenate([thirds((sampled.at[2], sampled.at[0])), thirds((sampled.at[1], sampled.at[3]))], axis=0).astype(BF)
     second_out = remote(s2.at[0], s2.at[1], 15, partner)
     second_out.start()
     third_out = []
@@ -475,7 +489,11 @@
         )
         copy.start()
         third_out.append(copy)
-
+    for copy in first_out + band_out[2:]:
+        copy.start()
+
+    for copy in small_loads:
+        copy.wait()
     line = lax.broadcasted_iota(jnp.int32, (D, D), 0)
     lane = lax.broadcasted_iota(jnp.int32, (D, D), 1)
     apart = jnp.abs(((lane - line + 64) & 127) - 64)
@@ -497,18 +515,37 @@
     @pl.when(jnp.logical_not(has_out))
     def _():
         halo_buf[0] = jnp.zeros((2, ROWS, D), BF)
-        halo_clause[0] = jnp.zeros((8, ROWS), jnp.int32)
+        halo_clause[0] = jnp.zeros((1, ROWS), jnp.int32)
 
     @pl.when(jnp.logical_not(has_beyond))
     def _():
         halo_buf[1] = jnp.zeros((2, ROWS, D), BF)
-        halo_clause[1] = jnp.zeros((8, ROWS), jnp.int32)
-
-    band_out[2].wait_recv()
-    band_out[3].wait_recv()
-
-    own = [ref[:, columns(c)] for ref in inputs]
-    other = [pair_buf[i] for i in range(4)]
+        halo_clause[1] = jnp.zeros((1, ROWS), jnp.int32)
+
+    second_out.wait_recv()
+    both = jnp.concatenate([s2[0], s2[1]], axis=0)
+    for h in range(2):
+        q, k, v, g = [both[:, (2 * i + h) * D : (2 * i + h + 1) * D] for i in range(4)]
+        results = softmax_grads(nt(q, k) * scale, q, k, v, g, scale)[:4]
+        for i in range(4):
+            second_ref[i, :, h * D : (h + 1) * D] = results[i][:32]
+
+    for copy in third_out:
+        copy.wait_recv()
+    blocks = [s3[i].astype(F32) for i in range(ctx_count)]
+    upper = jnp.concatenate([block[:8] for block in blocks], axis=0).astype(BF)
+    lower = jnp.concatenate([block[8:] for block in blocks], axis=0).astype(BF)
+    for h in range(2):
+        q, k = [upper[:, (2 * i + h) * D : (2 * i + h + 1) * D] for i in range(2)]
+        v, g = [lower[:, (2 * i + h) * D : (2 * i + h + 1) * D] for i in range(2)]
+        results = softmax_grads(nt(q, k) * scale, q, k, v, g, scale)[:4]
+        for i in range(4):
+            third_ref[i, :, h * D : (h + 1) * D] = results[i][:8]
+
+    for copy in loads:
+        copy.wait()
+    own = [local[i, 0] for i in range(4)]
+    other = [pair_buf[0], pair_buf[1]]
     clauses = {"own": clause_ref, "other": pair_clause}
     cols = {name: clause_column(ref) for name, ref in clauses.items()}
     hots = {name: one_hot(col) for name, col in cols.items()}
@@ -557,8 +594,16 @@
     attended, grad_q, gk_a, gv_a, pairs_a, rest_a = band_block(
         0, own, other, "own", "other", 1, has_out
     )
-    out_ref[0, c] = attended.astype(BF)
-    out_ref[1, c] = grad_q.astype(BF)
+    keeps = [
+        pltpu.make_async_copy(mine_send.at[i], out_ref.at[i, c], out_sem.at[i]) for i in range(8)
+    ]
+
+    def keep(i, value):
+        mine_send[i] = value.astype(BF)
+        keeps[i].start()
+
+    keep(0, attended)
+    keep(1, grad_q)
     grad_send[0, 0] = gk_a[2 * ROWS :].astype(BF)
     grad_send[0, 1] = gv_a[2 * ROWS :].astype(BF)
     back_out = remote(grad_send.at[0], grad_buf.at[0], 16, outward)
@@ -568,6 +613,22 @@
     def _():
         back_out.start()
 
+    ret = [remote(ret_send.at[i], out_ref.at[i, c], 18 + i, partner) for i in range(8)]
+    for copy in first_out:
+        copy.wait_recv()
+    k, v, q, g = [
+        jnp.concatenate([local[i, 1], pair_buf[4 + i]], axis=0) for i in range(4)
+    ]
+    results = softmax_grads(nt(q, k) * scale, q, k, v, g, scale)[:4]
+    for i in range(4):
+        ret_send[4 + i] = results[i][ROWS:].astype(BF)
+        ret[4 + i].start()
+        keep(4 + i, results[i][:ROWS])
+
+    band_out[2].wait_recv()
+    band_out[3].wait_recv()
+    other += [pair_buf[2], pair_buf[3]]
+
     @pl.when(has_beyond)
     def _():
         for copy in own_halo:
@@ -576,7 +637,6 @@
     attended, grad_q, gk_b, gv_b, pairs_b, rest_b = band_block(
         1, other, own, "other", "own", -1, has_beyond
     )
-    ret = [remote(ret_send.at[i], ret_buf.at[i], 18 + i, partner) for i in range(8)]
     ret_send[0] = attended.astype(BF)
     ret_send[1] = grad_q.astype(BF)
     grad_send[1, 0] = gk_b[2 * ROWS :].astype(BF)
@@ -619,17 +679,6 @@
         copy.start()
         bias_out.append(copy)
 
-    for copy in first_out:
-        copy.wait_recv()
-    k, v, q, g = [
-        jnp.concatenate([inputs[i][:, columns(2 + c)], pair_buf[4 + i]], axis=0) for i in range(4)
-    ]
-    results = softmax_grads(nt(q, k) * scale, q, k, v, g, scale)[:4]
-    for i in range(4):
-        out_ref[4 + i, c] = results[i][:ROWS].astype(BF)
-        ret_send[4 + i] = results[i][ROWS:].astype(BF)
-        ret[4 + i].start()
-
     @pl.when(has_beyond)
     def _():
         back_out.wait_recv()
@@ -637,9 +686,6 @@
     @pl.when(has_out)
     def _():
         back_far.wait_recv()
-
-    from_beyond = jnp.where(has_beyond, 1.0, 0.0)
-    from_out = jnp.where(has_out, 1.0, 0.0)
 
     @pl.when(jnp.logical_not(has_beyond))
     def _():
@@ -653,8 +699,8 @@
     ret_send[3] = (other_gv + grad_buf[0, 1].astype(F32)).astype(BF)
     ret[2].start()
     ret[3].start()
-    out_ref[2, c] = (own_gk + grad_buf[1, 0].astype(F32)).astype(BF)
-    out_ref[3, c] = (own_gv + grad_buf[1, 1].astype(F32)).astype(BF)
+    keep(2, own_gk + grad_buf[1, 0].astype(F32))
+    keep(3, own_gv + grad_buf[1, 1].astype(F32))
 
     for copy in bias_out:
         copy.wait_recv()
@@ -675,26 +721,6 @@
         copy.start()
         docs_out.append(copy)
 
-    second_out.wait_recv()
-    both = jnp.concatenate([s2[0], s2[1]], axis=0)
-    for h in range(2):
-        q, k, v, g = [both[:, (2 * i + h) * D : (2 * i + h + 1) * D] for i in range(4)]
-        results = softmax_grads(nt(q, k) * scale, q, k, v, g, scale)[:4]
-        for i in range(4):
-            second_ref[i, :, h * D : (h + 1) * D] = results[i][:32]
-
-    for copy in third_out:
-        copy.wait_recv()
-    blocks = [s3[i].astype(F32) for i in range(ctx_count)]
-    upper = jnp.concatenate([block[:8] for block in blocks], axis=0).astype(BF)
-    lower = jnp.concatenate([block[8:] for block in blocks], axis=0).astype(BF)
-    for h in range(2):
-        q, k = [upper[:, (2 * i + h) * D : (2 * i + h + 1) * D] for i in range(2)]
-        v, g = [lower[:, (2 * i + h) * D : (2 * i + h + 1) * D] for i in range(2)]
-        results = softmax_grads(nt(q, k) * scale, q, k, v, g, scale)[:4]
-        for i in range(4):
-            third_ref[i, :, h * D : (h + 1) * D] = results[i][:8]
-
     for copy in docs_out:
         copy.wait_recv()
     total = bias_dp[0]
@@ -702,9 +728,10 @@
         total = total + bias_dp[i]
     bias_ref[...] = total
 
-    for i in (4, 5, 6, 7, 0, 1, 2, 3):
-        ret[i].wait_recv()
-        out_ref[i, 1 - c] = ret_buf[i]
+    for copy in ret:
+        copy.wait_recv()
+    for copy in keeps:
+        copy.wait()
 
     for copy in band_out + first_out + [clause_out, second_out] + third_out + bias_out + docs_out + ret:
         copy.wait_send()
@@ -720,8 +747,14 @@
             copy.wait_send()
 
 
-def layout_kernel(heads_ref, second_ref, third_ref, *outs):
-    for i, out in enumerate(outs):
+def layout_kernel(heads_ref, second_ref, third_ref, tile_ref, *outs):
+    bias_ref = outs[4]
+    row = lax.broadcasted_iota(jnp.int32, (BUCKETS, D), 0)
+    col = lax.broadcasted_iota(jnp.int32, (BUCKETS, D), 1)
+    for h in range(2):
+        picked = jnp.where(row == col, tile_ref[h : h + 1, :], 0.0)
+        bias_ref[:, h : h + 1] = jnp.sum(picked, axis=1, keepdims=True)
+    for i, out in enumerate(outs[:4]):
         for h in range(2):
             out[:, h * D : (h + 1) * D] = heads_ref[i, h]
             out[:, (2 + h) * D : (3 + h) * D] = heads_ref[4 + i, h]
@@ -735,8 +768,7 @@
 
 def paired(ctx_count, dp_count, query, key, value, grad_out, clause, bias_table):
     vmem = pl.BlockSpec(memory_space=pltpu.VMEM)
-    smem = pl.BlockSpec(memory_space=pltpu.SMEM)
-    rows = jnp.broadcast_to(clause, (8, ROWS))
+    far = pl.BlockSpec(memory_space=pltpu.HBM)
     dma = pltpu.SemaphoreType.DMA
     block = (ROWS, D)
     heads, second, third, bias = pl.pallas_call(
@@ -747,16 +779,22 @@
             jax.ShapeDtypeStruct((4, 8, 2 * D), F32),
             jax.ShapeDtypeStruct((8, D), F32),
         ],
-        in_specs=[smem] + [vmem] * 5,
-        out_specs=[vmem] * 4,
+        in_specs=[far] * 6,
+        out_specs=[far] + [vmem] * 3,
         scratch_shapes=[
+            pltpu.SMEM((BUCKETS, 2), F32),
+            pltpu.VMEM((1, ROWS), jnp.int32),
+            pltpu.VMEM((4, 2) + block, BF),
+            pltpu.VMEM((4, ROWS, 4 * D), BF),
+            pltpu.VMEM((8,) + block, BF),
+            dma((14,)),
+            dma((8,)),
             pltpu.VMEM((8,) + block, BF),
             pltpu.VMEM((2, 2) + block, BF),
-            pltpu.VMEM((2, 8, ROWS), jnp.int32),
-            pltpu.VMEM((8, ROWS), jnp.int32),
+            pltpu.VMEM((2, 1, ROWS), jnp.int32),
+            pltpu.VMEM((1, ROWS), jnp.int32),
             pltpu.VMEM((2, 2) + block, BF),
             pltpu.VMEM((2, 2) + block, BF),
-            pltpu.VMEM((8,) + block, BF),
             pltpu.VMEM((8,) + block, BF),
             pltpu.VMEM((2, 32, 8 * D), BF),
             pltpu.VMEM((ctx_count, 16, 4 * D), BF),
@@ -775,16 +813,17 @@
             collective_id=0, has_side_effects=True, vmem_limit_bytes=48 * 1024 * 1024
         ),
         name="attend",
-    )(bias_table, rows, query[0], key[0], value[0], grad_out[0])
+    )(bias_table, clause, query[0], key[0], value[0], grad_out[0])
     outs = pl.pallas_call(
         layout_kernel,
-        out_shape=[jax.ShapeDtypeStruct((ROWS, HEADS * D), BF)] * 4,
-        in_specs=[vmem] * 3,
-        out_specs=[vmem] * 4,
+        out_shape=[jax.ShapeDtypeStruct((ROWS, HEADS * D), BF)] * 4
+        + [jax.ShapeDtypeStruct((BUCKETS, 2), F32)],
+        in_specs=[vmem] * 4,
+        out_specs=[vmem] * 5,
         compiler_params=pltpu.CompilerParams(vmem_limit_bytes=32 * 1024 * 1024),
         name="layout",
-    )(heads, second, third)
-    return tuple(out[None] for out in outs) + (bias[:2, :BUCKETS].T,)
+    )(heads, second, third, bias)
+    return tuple(out[None] for out in outs[:4]) + (outs[4],)
 
 
 def solution(mesh):

time: 43.4 us -> 44.6 us (1.028)
  Pallas kernels: 36.3 us -> 37.4 us
    pallas_call x1, Pallas kernels: 34.5 us -> 35.6 us  [paired(): pl.pallas_call(lambda *refs: main_kernel(ctx_count, dp_count, *refs), out...]
    transpose x1 -> x0, local copies, waits for them, and re-layouts: 0.56 us -> none  [paired(): return tuple((out[None] for out in outs)) + (bias[:2, :BUCKETS].T,)]
    unnamed x13 -> x14, local copies, waits for them, and re-layouts: 5.6 us -> 6.15 us
where the time goes in v2:
time: 44.6 us; the launch traced here: 44.2 us
  Pallas kernels  37.4 us (84%)
  local copies, waits for them, and re-layouts  6.15 us (14%)
  between operations  0.65 us (1%)
    pallas_call x1, Pallas kernels, paired(): pl.pallas_call(lambda *refs: main_kernel(ctx_count, dp_count, *refs), out...  35.6 us
    unnamed x14, local copies, waits for them, and re-layouts  6.15 us
    pallas_call x1, Pallas kernels, paired(): pl.pallas_call(layout_kernel, out_shape=[jax.ShapeDtypeStruct((ROWS, HEAD...  1.79 us

profile of v2, /device:TPU:0, one launch (start us, length us, event | category | flops | bytes accessed | tf_op | source)
XLA Modules:
  0.0 44.2 jit_solution(6010125773666067431)
XLA Ops:
  0.6 0.0 copy-start.5
  0.6 0.7 %copy-done.5 = f32[32,2]{0,1:T(2,128)S(1)} copy-done((f32[32,2]{0,1:T(2,128)S(1)}, f32[32,2]{0,1:T(2,128)}, u32[]{:S(2)}) %copy-start.5) | copy-done | bytes 280
  1.3 0.0 copy-start.4
  1.3 0.1 copy.11.refs_0_
  1.4 0.6 %copy-done.4 = s32[1,256]{1,0:T(1,128)S(1)} copy-done((s32[1,256]{1,0:T(1,128)S(1)}, s32[1,256]{1,0:T(1,128)}, u32[]{:S(2)}) %copy-start.4) | copy-done | bytes 1048
  2.0 0.0 copy-start
  2.0 1.0 %copy-done = bf16[1,256,1024]{2,1,0:T(8,128)(2,1)S(1)} copy-done((bf16[1,256,1024]{2,1,0:T(8,128)(2,1)S(1)}, bf16[1,256,1024]{2,1,0:T(8,128)(2,1)}, u32[]{:S(2)}) %copy-start) | copy-done | bytes 524312
  3.0 0.0 copy-start.1
  3.0 1.0 %copy-done.1 = bf16[1,256,1024]{2,1,0:T(8,128)(2,1)S(1)} copy-done((bf16[1,256,1024]{2,1,0:T(8,128)(2,1)S(1)}, bf16[1,256,1024]{2,1,0:T(8,128)(2,1)}, u32[]{:S(2)}) %copy-start.1) | copy-done | bytes 524312
  4.1 0.0 copy-start.2
  4.1 1.0 %copy-done.2 = bf16[1,256,1024]{2,1,0:T(8,128)(2,1)S(1)} copy-done((bf16[1,256,1024]{2,1,0:T(8,128)(2,1)S(1)}, bf16[1,256,1024]{2,1,0:T(8,128)(2,1)}, u32[]{:S(2)}) %copy-start.2) | copy-done | bytes 524312
  5.1 0.0 copy-start.3
  5.1 1.0 %copy-done.3 = bf16[1,256,1024]{2,1,0:T(8,128)(2,1)S(1)} copy-done((bf16[1,256,1024]{2,1,0:T(8,128)(2,1)S(1)}, bf16[1,256,1024]{2,1,0:T(8,128)(2,1)}, u32[]{:S(2)}) %copy-start.3) | copy-done | bytes 524312
  6.2 35.6 %attend.1 = (bf16[8,2,256,128]{3,2,1,0:T(8,128)(2,1)S(1)}, f32[4,32,256]{2,1,0:T(8,128)S(1)}, f32[4,8,256]{2,1,0:T(8,128)S(1)}, f32[8,128]{1,0:T(8,128)S(1)}) custom-call(f32[32,2]{1,0:T(8,128)S(1)} %copy.11.refs_0_, s32[1,256]{1,0:T(1,128)S(1)} %copy-done.4, bf16[256,1024]{1,0:T(8,128)(2,1)S(1)} %bitcast.8, bf16[256,1024]{1,0:T(8,128)(2,1)S(1)} %bitcast.9, ...), custom_call_target="tpu_custom_call" | custom-call | tf_op jit(solution)/shard_map/attend/pallas_call | solution.py:774
  41.8 1.8 %layout.1 = (bf16[256,1024]{1,0:T(8,128)(2,1)}, bf16[256,1024]{1,0:T(8,128)(2,1)}, bf16[256,1024]{1,0:T(8,128)(2,1)}, bf16[256,1024]{1,0:T(8,128)(2,1)}, f32[32,2]{1,0:T(8,128)S(1)}) custom-call(bf16[8,2,256,128]{3,2,1,0:T(8,128)(2,1)S(1)} %get-tuple-element.14.heads_ref, f32[4,32,256]{2,1,0:T(8,128)S(1)} %get-tuple-element.15.second_ref, ...), custom_call_target="tpu_custom_call" | custom-call | tf_op jit(solution)/shard_map/layout/pallas_call | solution.py:817
  43.6 0.6 %copy.12 = f32[32,2]{0,1:T(2,128)} copy(f32[32,2]{1,0:T(8,128)S(1)} %get-tuple-element.27) | data formatting | bytes 512
Async XLA Ops:
  0.6 0.7 %copy-start.5 = (f32[32,2]{0,1:T(2,128)S(1)}, f32[32,2]{0,1:T(2,128)}, u32[]{:S(2)}) copy-start(f32[32,2]{0,1:T(2,128)} %param.11) | copy-start | bytes 772
  1.3 0.7 %copy-start.4 = (s32[1,256]{1,0:T(1,128)S(1)}, s32[1,256]{1,0:T(1,128)}, u32[]{:S(2)}) copy-start(s32[1,256]{1,0:T(1,128)} %refs_1_.1) | copy-start | bytes 3076
  2.0 1.0 %copy-start = (bf16[1,256,1024]{2,1,0:T(8,128)(2,1)S(1)}, bf16[1,256,1024]{2,1,0:T(8,128)(2,1)}, u32[]{:S(2)}) copy-start(bf16[1,256,1024]{2,1,0:T(8,128)(2,1)} %param.6) | copy-start | bytes 1572868
  3.0 1.0 %copy-start.1 = (bf16[1,256,1024]{2,1,0:T(8,128)(2,1)S(1)}, bf16[1,256,1024]{2,1,0:T(8,128)(2,1)}, u32[]{:S(2)}) copy-start(bf16[1,256,1024]{2,1,0:T(8,128)(2,1)} %param.7) | copy-start | bytes 1572868
  4.1 1.0 %copy-start.2 = (bf16[1,256,1024]{2,1,0:T(8,128)(2,1)S(1)}, bf16[1,256,1024]{2,1,0:T(8,128)(2,1)}, u32[]{:S(2)}) copy-start(bf16[1,256,1024]{2,1,0:T(8,128)(2,1)} %param.8) | copy-start | bytes 1572868
  5.1 1.0 %copy-start.3 = (bf16[1,256,1024]{2,1,0:T(8,128)(2,1)S(1)}, bf16[1,256,1024]{2,1,0:T(8,128)(2,1)}, u32[]{:S(2)}) copy-start(bf16[1,256,1024]{2,1,0:T(8,128)(2,1)} %param.9) | copy-start | bytes 1572868

commit v3 on v2

--- a/solution.py
+++ b/solution.py
@@ -347,6 +347,21 @@
     return attended, grad_q, grad_k, grad_v, logit_grads
 
 
+def softmax_rows(rows, chunk, score_ref, grad_ref, weight_ref, score_grad_ref, shape_scores, take_grads):
+    for start in range(0, rows, chunk):
+        at = pl.ds(start, chunk)
+        scores = shape_scores(at, start, score_ref[at, :])
+        top = jnp.max(scores, axis=-1, keepdims=True)
+        raised = jnp.exp(scores - top)
+        shares = raised * (1.0 / jnp.sum(raised, axis=-1, keepdims=True))
+        weight_ref[at, :] = shares.astype(BF)
+        weight_grads = grad_ref[at, :]
+        delta = jnp.sum(shares * weight_grads, axis=-1, keepdims=True)
+        logit_grads = shares * (weight_grads - delta)
+        score_grad_ref[at, :] = logit_grads.astype(BF)
+        take_grads(at, logit_grads)
+
+
 def selector(count, step, offset):
     row = lax.broadcasted_iota(jnp.int32, (count, ROWS), 0)
     col = lax.broadcasted_iota(jnp.int32, (count, ROWS), 1)
@@ -375,6 +390,7 @@
     table_ref, clause_ref, local, sampled, mine_send, local_sem, out_sem,
     pair_buf, halo_buf, halo_clause, pair_clause, grad_buf, grad_send, ret_send,
     s2, s3, bias_ctx, bias_dp,
+    band_scores, band_bias, band_wg, band_w, band_sg, band_high, band_low, pair_scores, pair_wg, pair_w, pair_sg,
     send_sem, recv_sem, s3_send, s3_recv, bc_send, bc_recv, bd_send, bd_recv,
 ):
     me = lax.axis_index("ctx")
@@ -477,18 +493,15 @@
     s3[0] = jnp.concatenate([thirds((sampled.at[2], sampled.at[0])), thirds((sampled.at[1], sampled.at[3]))], axis=0).astype(BF)
     second_out = remote(s2.at[0], s2.at[1], 15, partner)
     second_out.start()
-    third_out = []
-    for step in range(1, ctx_count):
-        copy = pltpu.make_async_remote_copy(
-            src_ref=s3.at[0],
-            dst_ref=s3.at[ctx_count - step],
-            send_sem=s3_send.at[step],
-            recv_sem=s3_recv.at[ctx_count - step],
-            device_id=(row, lax.rem(me + step, ctx_count)),
-            device_id_type=mesh_id,
-        )
-        copy.start()
-        third_out.append(copy)
+    third_pair = pltpu.make_async_remote_copy(
+        src_ref=s3.at[0],
+        dst_ref=s3.at[1],
+        send_sem=s3_send.at[0],
+        recv_sem=s3_recv.at[0],
+        device_id=(row, partner),
+        device_id_type=mesh_id,
+    )
+    third_pair.start()
     for copy in first_out + band_out[2:]:
         copy.start()
 
@@ -499,8 +512,8 @@
     apart = jnp.abs(((lane - line + 64) & 127) - 64)
     table = jnp.zeros((D, D), F32)
     for level in range(BUCKETS):
-        table = jnp.where(apart == level, table_ref[level, c], table)
-    far_bias = table_ref[BUCKETS - 1, c]
+        table = jnp.where(apart == level, table_ref[c, level], table)
+    far_bias = table_ref[c, BUCKETS - 1]
     table_high, table_low = halves(table)
 
     clause_out.wait_recv()
@@ -521,6 +534,20 @@
     def _():
         halo_buf[1] = jnp.zeros((2, ROWS, D), BF)
         halo_clause[1] = jnp.zeros((1, ROWS), jnp.int32)
+
+    third_pair.wait_recv()
+    third_out = []
+    for step in range(1, ctx_count // 2):
+        copy = pltpu.make_async_remote_copy(
+            src_ref=s3.at[pl.ds(0, 2)],
+            dst_ref=s3.at[pl.ds(ctx_count - 2 * step, 2)],
+            send_sem=s3_send.at[step],
+            recv_sem=s3_recv.at[step],
+            device_id=(row, lax.rem(me + 2 * step, ctx_count)),
+            device_id_type=mesh_id,
+        )
+        copy.start()
+        third_out.append(copy)
 
     second_out.wait_recv()
     both = jnp.concatenate([s2[0], s2[1]], axis=0)
@@ -549,10 +576,6 @@
     clauses = {"own": clause_ref, "other": pair_clause}
     cols = {name: clause_column(ref) for name, ref in clauses.items()}
     hots = {name: one_hot(col) for name, col in cols.items()}
-    line = lax.broadcasted_iota(jnp.int32, (ROWS, ROWS), 0)
-    lane = lax.broadcasted_iota(jnp.int32, (ROWS, ROWS), 1)
-    diff = (line - lane) * (1 - 2 * c)
-
     def band_block(slot, mine, near, mine_name, near_name, sign, halo_valid):
         k = jnp.concatenate([mine[0], near[0], halo_buf[slot, 0]], axis=0)
         v = jnp.concatenate([mine[1], near[1], halo_buf[slot, 1]], axis=0)
@@ -564,34 +587,57 @@
             axis=1,
         )
         query_hot = hots[mine_name]
-        close = jnp.abs(cols[mine_name][:, 0:1] - key_row) < BUCKETS - 1
         spread = jnp.concatenate(
             [nn(query_hot, table_high).astype(BF), nn(query_hot, table_low).astype(BF)], axis=1
         )
-        bias = nt(spread, jnp.concatenate([key_hot, key_hot], axis=1))
-        signed = diff * sign
+        band_bias[...] = nt(spread, jnp.concatenate([key_hot, key_hot], axis=1))
+        band_scores[...] = nt(q, k)
+        band_wg[...] = nt(g, v)
         reach = jnp.where(halo_valid, 0, ROWS)
-        allowed = jnp.concatenate(
-            [jnp.ones((ROWS, ROWS), jnp.int32), jnp.where(signed > 0, 1, 0), jnp.where(-signed > reach, 1, 0)],
-            axis=1,
-        )
-        scores = nt(q, k) * scale + jnp.where(close, bias, far_bias)
-        scores = jnp.where(allowed > 0, scores, -jnp.inf)
-        attended, grad_q, grad_k, grad_v, logit_grads = softmax_grads(scores, q, k, v, g, scale)
-        kept = jnp.where(close, logit_grads, 0.0)
-        rest = jnp.sum(jnp.where(close, 0.0, logit_grads), axis=0, keepdims=True)
-        high, low = halves(kept)
-        by_clause = nn(high, key_hot) + nn(low, key_hot)
+        col = cols[mine_name]
+        turn = (1 - 2 * c) * sign
+        chunk = 32
+
+        def near_clauses(start):
+            return jnp.abs(col[start : start + chunk, 0:1] - key_row) < BUCKETS - 1
+
+        def shape_scores(at, start, scores):
+            close = near_clauses(start)
+            scores = scores * scale + jnp.where(close, band_bias[at, :], far_bias)
+            row_index = lax.broadcasted_iota(jnp.int32, (chunk, ROWS), 0) + start
+            col_index = lax.broadcasted_iota(jnp.int32, (chunk, ROWS), 1)
+            signed = (row_index - col_index) * turn
+            return jnp.concatenate(
+                [
+                    scores[:, :ROWS],
+                    jnp.where(signed > 0, scores[:, ROWS : 2 * ROWS], -jnp.inf),
+                    jnp.where(-signed > reach, scores[:, 2 * ROWS :], -jnp.inf),
+                ],
+                axis=1,
+            )
+
+        def take_grads(at, logit_grads):
+            high, low = halves(jnp.where(near_clauses(at.start), logit_grads, 0.0))
+            band_high[at, :] = high
+            band_low[at, :] = low
+
+        softmax_rows(ROWS, chunk, band_scores, band_wg, band_w, band_sg, shape_scores, take_grads)
+        weights, score_grads = band_w[...], band_sg[...]
+        attended = nn(weights, v)
+        grad_q = nn(score_grads, k) * scale
+        grad_k = tn(score_grads, q) * scale
+        grad_v = tn(weights, g)
+        by_clause = nn(band_high[...], key_hot) + nn(band_low[...], key_hot)
         high, low = halves(by_clause)
         pairs = tn(query_hot, high) + tn(query_hot, low) + tn(high, query_hot) + tn(low, query_hot)
-        return attended, grad_q, grad_k, grad_v, pairs, rest
+        return attended, grad_q, grad_k, grad_v, pairs
 
     @pl.when(has_out)
     def _():
         for copy in far_halo:
             copy.wait_recv()
 
-    attended, grad_q, gk_a, gv_a, pairs_a, rest_a = band_block(
+    attended, grad_q, gk_a, gv_a, pairs_a = band_block(
         0, own, other, "own", "other", 1, has_out
     )
     keeps = [
@@ -619,7 +665,16 @@
     k, v, q, g = [
         jnp.concatenate([local[i, 1], pair_buf[4 + i]], axis=0) for i in range(4)
     ]
-    results = softmax_grads(nt(q, k) * scale, q, k, v, g, scale)[:4]
+    pair_scores[...] = nt(q, k)
+    pair_wg[...] = nt(g, v)
+    softmax_rows(
+        2 * ROWS, 32, pair_scores, pair_wg, pair_w, pair_sg,
+        lambda at, start, scores: scores * scale, lambda at, logit_grads: None,
+    )
+    weights, score_grads = pair_w[...], pair_sg[...]
+    results = (
+        nn(weights, v), nn(score_grads, k) * scale, tn(score_grads, q) * scale, tn(weights, g)
+    )
     for i in range(4):
         ret_send[4 + i] = results[i][ROWS:].astype(BF)
         ret[4 + i].start()
@@ -634,7 +689,7 @@
         for copy in own_halo:
             copy.wait_recv()
 
-    attended, grad_q, gk_b, gv_b, pairs_b, rest_b = band_block(
+    attended, grad_q, gk_b, gv_b, pairs_b = band_block(
         1, other, own, "other", "own", -1, has_beyond
     )
     ret_send[0] = attended.astype(BF)
@@ -660,10 +715,10 @@
         rolled = jnp.concatenate([turned[:, shift:], turned[:, :shift]], axis=1)
         turned = jnp.where((line & shift) > 0, rolled, turned)
     sums = jnp.sum(turned, axis=0, keepdims=True)
-    rest = jnp.sum(rest_a + rest_b, axis=1, keepdims=True)
     lane = lax.broadcasted_iota(jnp.int32, (1, D), 1)
     sums = jnp.where(lane == 0, 0.5 * sums, sums)
-    sums = jnp.where(lane < BUCKETS - 1, sums, jnp.where(lane == BUCKETS - 1, rest, 0.0))
+    sums = jnp.where(lane < BUCKETS - 1, sums, 0.0)
+    sums = jnp.where(lane == BUCKETS - 1, -jnp.sum(sums, axis=1, keepdims=True), sums)
     tile_line = lax.broadcasted_iota(jnp.int32, (8, D), 0)
     bias_ctx[me] = jnp.where(tile_line == c, sums, 0.0)
     bias_out = []
@@ -733,7 +788,7 @@
     for copy in keeps:
         copy.wait()
 
-    for copy in band_out + first_out + [clause_out, second_out] + third_out + bias_out + docs_out + ret:
+    for copy in band_out + first_out + [clause_out, second_out, third_pair] + third_out + bias_out + docs_out + ret:
         copy.wait_send()
 
     @pl.when(has_out)
@@ -748,12 +803,7 @@
 
 
 def layout_kernel(heads_ref, second_ref, third_ref, tile_ref, *outs):
-    bias_ref = outs[4]
-    row = lax.broadcasted_iota(jnp.int32, (BUCKETS, D), 0)
-    col = lax.broadcasted_iota(jnp.int32, (BUCKETS, D), 1)
-    for h in range(2):
-        picked = jnp.where(row == col, tile_ref[h : h + 1, :], 0.0)
-        bias_ref[:, h : h + 1] = jnp.sum(picked, axis=1, keepdims=True)
+    outs[4][...] = tile_ref[0:2, 0:BUCKETS]
     for i, out in enumerate(outs[:4]):
         for h in range(2):
             out[:, h * D : (h + 1) * D] = heads_ref[i, h]
@@ -782,7 +832,7 @@
         in_specs=[far] * 6,
         out_specs=[far] + [vmem] * 3,
         scratch_shapes=[
-            pltpu.SMEM((BUCKETS, 2), F32),
+            pltpu.SMEM((2, BUCKETS), F32),
             pltpu.VMEM((1, ROWS), jnp.int32),
             pltpu.VMEM((4, 2) + block, BF),
             pltpu.VMEM((4, ROWS, 4 * D), BF),
@@ -800,6 +850,17 @@
             pltpu.VMEM((ctx_count, 16, 4 * D), BF),
             pltpu.VMEM((ctx_count, 8, D), F32),
             pltpu.VMEM((dp_count, 8, D), F32),
+            pltpu.VMEM((ROWS, 3 * ROWS), F32),
+            pltpu.VMEM((ROWS, 3 * ROWS), F32),
+            pltpu.VMEM((ROWS, 3 * ROWS), F32),
+            pltpu.VMEM((ROWS, 3 * ROWS), BF),
+            pltpu.VMEM((ROWS, 3 * ROWS), BF),
+            pltpu.VMEM((ROWS, 3 * ROWS), BF),
+            pltpu.VMEM((ROWS, 3 * ROWS), BF),
+            pltpu.VMEM((2 * ROWS, 2 * ROWS), F32),
+            pltpu.VMEM((2 * ROWS, 2 * ROWS), F32),
+            pltpu.VMEM((2 * ROWS, 2 * ROWS), BF),
+            pltpu.VMEM((2 * ROWS, 2 * ROWS), BF),
             dma((26,)),
             dma((26,)),
             dma((ctx_count,)),
@@ -810,20 +871,20 @@
             dma((dp_count,)),
         ],
         compiler_params=pltpu.CompilerParams(
-            collective_id=0, has_side_effects=True, vmem_limit_bytes=48 * 1024 * 1024
+            collective_id=0, has_side_effects=True, vmem_limit_bytes=64 * 1024 * 1024
         ),
         name="attend",
-    )(bias_table, clause, query[0], key[0], value[0], grad_out[0])
+    )(bias_table.T, clause, query[0], key[0], value[0], grad_out[0])
     outs = pl.pallas_call(
         layout_kernel,
         out_shape=[jax.ShapeDtypeStruct((ROWS, HEADS * D), BF)] * 4
-        + [jax.ShapeDtypeStruct((BUCKETS, 2), F32)],
+        + [jax.ShapeDtypeStruct((2, BUCKETS), F32)],
         in_specs=[vmem] * 4,
         out_specs=[vmem] * 5,
-        compiler_params=pltpu.CompilerParams(vmem_limit_bytes=32 * 1024 * 1024),
+        compiler_params=pltpu.CompilerParams(vmem_limit_bytes=64 * 1024 * 1024),
         name="layout",
     )(heads, second, third, bias)
-    return tuple(out[None] for out in outs[:4]) + (outs[4],)
+    return tuple(out[None] for out in outs[:4]) + (outs[4].T,)
 
 
 def solution(mesh):

time: 44.6 us -> 39.9 us (0.89)
  local copies, waits for them, and re-layouts: 6.15 us -> 0 us
  Pallas kernels: 37.4 us -> 39.1 us
    unnamed x14 -> x0, local copies, waits for them, and re-layouts: 6.15 us -> none
    pallas_call x1, Pallas kernels: 1.79 us -> 3.09 us  [paired(): pl.pallas_call(layout_kernel, out_shape=[jax.ShapeDtypeStruct((ROWS, HEAD...]
where the time goes in v3:
time: 39.9 us; the launch traced here: 39.8 us
  Pallas kernels  39.1 us (98%)
  between operations  0.64 us (2%)
    pallas_call x1, Pallas kernels, paired(): pl.pallas_call(lambda *refs: main_kernel(ctx_count, dp_count, *refs), out...  36.1 us
    pallas_call x1, Pallas kernels, paired(): pl.pallas_call(layout_kernel, out_shape=[jax.ShapeDtypeStruct((ROWS, HEAD...  3.09 us

profile of v3, /device:TPU:0, one launch (start us, length us, event | category | flops | bytes accessed | tf_op | source)
XLA Modules:
  0.0 39.8 jit_solution(4931204087620143032)
XLA Ops:
  0.6 36.1 %attend.1 = (bf16[8,2,256,128]{3,2,1,0:T(8,128)(2,1)}, f32[4,32,256]{2,1,0:T(8,128)}, f32[4,8,256]{2,1,0:T(8,128)}, f32[8,128]{1,0:T(8,128)}) custom-call(f32[2,32]{1,0:T(2,128)} %bitcast.14, s32[1,256]{1,0:T(1,128)} %refs_1_.1, bf16[256,1024]{1,0:T(8,128)(2,1)} %bitcast.10, bf16[256,1024]{1,0:T(8,128)(2,1)} %bitcast.11, bf16[256,1024]{1,0:T(8,128)(2,1)} %bitcast.12, ...), custom_call_target="tpu_custom_call" | custom-call | tf_op jit(solution)/shard_map/attend/pallas_call | solution.py:824
  36.7 3.1 %layout.1 = (bf16[256,1024]{1,0:T(8,128)(2,1)}, bf16[256,1024]{1,0:T(8,128)(2,1)}, bf16[256,1024]{1,0:T(8,128)(2,1)}, bf16[256,1024]{1,0:T(8,128)(2,1)}, f32[2,32]{1,0:T(2,128)}) custom-call(bf16[8,2,256,128]{3,2,1,0:T(8,128)(2,1)} %get-tuple-element.14.heads_ref, f32[4,32,256]{2,1,0:T(8,128)} %get-tuple-element.15.second_ref, ...), custom_call_target="tpu_custom_call" | custom-call | tf_op jit(solution)/shard_map/layout/pallas_call | solution.py:878

commit v4 on v3

--- a/solution.py
+++ b/solution.py
@@ -386,8 +386,8 @@
 def main_kernel(
     ctx_count, dp_count,
     table_hbm, clause_hbm, q_ref, k_ref, v_ref, g_ref,
-    out_ref, second_ref, third_ref, bias_ref,
-    table_ref, clause_ref, local, sampled, mine_send, local_sem, out_sem,
+    out_ref, second_out_ref, third_out_ref, bias_ref,
+    second_ref, third_ref, table_ref, clause_ref, local, sampled, mine_send, local_sem, out_sem,
     pair_buf, halo_buf, halo_clause, pair_clause, grad_buf, grad_send, ret_send,
     s2, s3, bias_ctx, bias_dp,
     band_scores, band_bias, band_wg, band_w, band_sg, band_high, band_low, pair_scores, pair_wg, pair_w, pair_sg,
@@ -409,17 +409,17 @@
 
     inputs = (k_ref, v_ref, q_ref, g_ref)
     loads = [
-        pltpu.make_async_copy(ref.at[:, columns(2 * j + c)], local.at[i, j], local_sem.at[2 * i + j])
+        pltpu.make_async_copy(ref.at[:, columns(head)], local.at[i, j], local_sem.at[3 * i + j])
         for i, ref in enumerate(inputs)
-        for j in range(2)
+        for j, head in enumerate((c, 2, 3))
     ]
     sample_loads = [
-        pltpu.make_async_copy(ref.at[:, 4 * D :], sampled.at[i], local_sem.at[8 + i])
+        pltpu.make_async_copy(ref.at[:, 4 * D :], sampled.at[i], local_sem.at[12 + i])
         for i, ref in enumerate(inputs)
     ]
     small_loads = [
-        pltpu.make_async_copy(clause_hbm, clause_ref, local_sem.at[12]),
-        pltpu.make_async_copy(table_hbm, table_ref, local_sem.at[13]),
+        pltpu.make_async_copy(clause_hbm, clause_ref, local_sem.at[16]),
+        pltpu.make_async_copy(table_hbm, table_ref, local_sem.at[17]),
     ]
     for copy in sample_loads + small_loads + loads:
         copy.start()
@@ -449,7 +449,8 @@
         remote(inputs[i].at[:, columns(1 - c)], pair_buf.at[i], i, partner) for i in range(4)
     ]
     first_out = [
-        remote(inputs[i].at[:, columns(3 - c)], pair_buf.at[4 + i], 4 + i, partner)
+        remote(inputs[i].at[:, columns(2 + h)], pair_buf.at[4 + 4 * h + i], 18 + 4 * h + i, partner)
+        for h in range(2)
         for i in range(4)
     ]
     clause_out = remote(clause_hbm, pair_clause, 8, partner)
@@ -502,7 +503,7 @@
         device_id_type=mesh_id,
     )
     third_pair.start()
-    for copy in first_out + band_out[2:]:
+    for copy in band_out[2:] + first_out[:4]:
         copy.start()
 
     for copy in small_loads:
@@ -569,6 +570,12 @@
         for i in range(4):
             third_ref[i, :, h * D : (h + 1) * D] = results[i][:8]
 
+    smalls = [
+        pltpu.make_async_copy(second_ref, second_out_ref, out_sem.at[12]),
+        pltpu.make_async_copy(third_ref, third_out_ref, out_sem.at[13]),
+    ]
+    for copy in smalls:
+        copy.start()
     for copy in loads:
         copy.wait()
     own = [local[i, 0] for i in range(4)]
@@ -641,7 +648,11 @@
         0, own, other, "own", "other", 1, has_out
     )
     keeps = [
-        pltpu.make_async_copy(mine_send.at[i], out_ref.at[i, c], out_sem.at[i]) for i in range(8)
+        pltpu.make_async_copy(mine_send.at[i], out_ref.at[i, c], out_sem.at[i]) for i in range(4)
+    ] + [
+        pltpu.make_async_copy(mine_send.at[4 + 4 * h + i], out_ref.at[4 + i, h], out_sem.at[4 + 4 * h + i])
+        for h in range(2)
+        for i in range(4)
     ]
 
     def keep(i, value):
@@ -659,27 +670,9 @@
     def _():
         back_out.start()
 
-    ret = [remote(ret_send.at[i], out_ref.at[i, c], 18 + i, partner) for i in range(8)]
-    for copy in first_out:
-        copy.wait_recv()
-    k, v, q, g = [
-        jnp.concatenate([local[i, 1], pair_buf[4 + i]], axis=0) for i in range(4)
-    ]
-    pair_scores[...] = nt(q, k)
-    pair_wg[...] = nt(g, v)
-    softmax_rows(
-        2 * ROWS, 32, pair_scores, pair_wg, pair_w, pair_sg,
-        lambda at, start, scores: scores * scale, lambda at, logit_grads: None,
-    )
-    weights, score_grads = pair_w[...], pair_sg[...]
-    results = (
-        nn(weights, v), nn(score_grads, k) * scale, tn(score_grads, q) * scale, tn(weights, g)
-    )
-    for i in range(4):
-        ret_send[4 + i] = results[i][ROWS:].astype(BF)
-        ret[4 + i].start()
-        keep(4 + i, results[i][:ROWS])
-
+    ret = [remote(ret_send.at[i], out_ref.at[i, c], 4 + i, partner) for i in range(4)]
+    for copy in first_out[4:]:
+        copy.start()
     band_out[2].wait_recv()
     band_out[3].wait_recv()
     other += [pair_buf[2], pair_buf[3]]
@@ -734,6 +727,25 @@
         copy.start()
         bias_out.append(copy)
 
+    def first_group(h):
+        for copy in first_out[4 * h : 4 * h + 4]:
+            copy.wait_recv()
+        k, v, q, g = [
+            jnp.concatenate([local[i, 1 + h], pair_buf[4 + 4 * h + i]], axis=0) for i in range(4)
+        ]
+        pair_scores[...] = nt(q, k)
+        pair_wg[...] = nt(g, v)
+        softmax_rows(
+            2 * ROWS, 32, pair_scores, pair_wg, pair_w, pair_sg,
+            lambda at, start, scores: scores * scale, lambda at, logit_grads: None,
+        )
+        keep(4 + 4 * h, nn(pair_w[:ROWS, :], v))
+        keep(5 + 4 * h, nn(pair_sg[:ROWS, :], k) * scale)
+        keep(6 + 4 * h, tn(pair_sg[:, :ROWS], q) * scale)
+        keep(7 + 4 * h, tn(pair_w[:, :ROWS], g))
+
+    first_group(0)
+
     @pl.when(has_beyond)
     def _():
         back_out.wait_recv()
@@ -776,6 +788,8 @@
         copy.start()
         docs_out.append(copy)
 
+    first_group(1)
+
     for copy in docs_out:
         copy.wait_recv()
     total = bias_dp[0]
@@ -785,7 +799,7 @@
 
     for copy in ret:
         copy.wait_recv()
-    for copy in keeps:
+    for copy in keeps + smalls:
         copy.wait()
 
     for copy in band_out + first_out + [clause_out, second_out, third_pair] + third_out + bias_out + docs_out + ret:
@@ -802,18 +816,30 @@
             copy.wait_send()
 
 
-def layout_kernel(heads_ref, second_ref, third_ref, tile_ref, *outs):
-    outs[4][...] = tile_ref[0:2, 0:BUCKETS]
-    for i, out in enumerate(outs[:4]):
+def layout_kernel(heads_hbm, second_ref, third_ref, tile_ref, *refs):
+    outs, bias_ref, heads, full, in_sem, out_sem = refs[:4], refs[4], *refs[5:]
+    loads = [pltpu.make_async_copy(heads_hbm.at[i], heads.at[i], in_sem.at[i]) for i in range(8)]
+    stores = [pltpu.make_async_copy(full.at[i], outs[i], out_sem.at[i]) for i in range(4)]
+    for i in range(4):
+        loads[i].start()
+        loads[4 + i].start()
+    bias_ref[...] = tile_ref[0:2, 0:BUCKETS]
+    for i in range(4):
         for h in range(2):
-            out[:, h * D : (h + 1) * D] = heads_ref[i, h]
-            out[:, (2 + h) * D : (3 + h) * D] = heads_ref[4 + i, h]
             seconds = second_ref[i, :, h * D : (h + 1) * D].astype(BF)
             spread = tn(selector(32, DILATION_SECOND, h * DILATION_SECOND // 2), seconds)
-            out[:, (4 + h) * D : (5 + h) * D] = spread.astype(BF)
+            full[i, :, (4 + h) * D : (5 + h) * D] = spread.astype(BF)
             thirds = third_ref[i, :, h * D : (h + 1) * D].astype(BF)
             spread = tn(selector(8, DILATION_THIRD, h * DILATION_THIRD // 2), thirds)
-            out[:, (6 + h) * D : (7 + h) * D] = spread.astype(BF)
+            full[i, :, (6 + h) * D : (7 + h) * D] = spread.astype(BF)
+        loads[i].wait()
+        loads[4 + i].wait()
+        for h in range(2):
+            full[i, :, h * D : (h + 1) * D] = heads[i, h]
+            full[i, :, (2 + h) * D : (3 + h) * D] = heads[4 + i, h]
+        stores[i].start()
+    for copy in stores:
+        copy.wait()
 
 
 def paired(ctx_count, dp_count, query, key, value, grad_out, clause, bias_table):
@@ -830,22 +856,24 @@
             jax.ShapeDtypeStruct((8, D), F32),
         ],
         in_specs=[far] * 6,
-        out_specs=[far] + [vmem] * 3,
+        out_specs=[far] * 3 + [vmem],
         scratch_shapes=[
+            pltpu.VMEM((4, 32, 2 * D), F32),
+            pltpu.VMEM((4, 8, 2 * D), F32),
             pltpu.SMEM((2, BUCKETS), F32),
             pltpu.VMEM((1, ROWS), jnp.int32),
-            pltpu.VMEM((4, 2) + block, BF),
+            pltpu.VMEM((4, 3) + block, BF),
             pltpu.VMEM((4, ROWS, 4 * D), BF),
-            pltpu.VMEM((8,) + block, BF),
+            pltpu.VMEM((12,) + block, BF),
+            dma((18,)),
             dma((14,)),
-            dma((8,)),
-            pltpu.VMEM((8,) + block, BF),
+            pltpu.VMEM((12,) + block, BF),
             pltpu.VMEM((2, 2) + block, BF),
             pltpu.VMEM((2, 1, ROWS), jnp.int32),
             pltpu.VMEM((1, ROWS), jnp.int32),
             pltpu.VMEM((2, 2) + block, BF),
             pltpu.VMEM((2, 2) + block, BF),
-            pltpu.VMEM((8,) + block, BF),
+            pltpu.VMEM((4,) + block, BF),
             pltpu.VMEM((2, 32, 8 * D), BF),
             pltpu.VMEM((ctx_count, 16, 4 * D), BF),
             pltpu.VMEM((ctx_count, 8, D), F32),
@@ -879,8 +907,14 @@
         layout_kernel,
         out_shape=[jax.ShapeDtypeStruct((ROWS, HEADS * D), BF)] * 4
         + [jax.ShapeDtypeStruct((2, BUCKETS), F32)],
-        in_specs=[vmem] * 4,
-        out_specs=[vmem] * 5,
+        in_specs=[far] + [vmem] * 3,
+        out_specs=[far] * 4 + [vmem],
+        scratch_shapes=[
+            pltpu.VMEM((8, 2) + block, BF),
+            pltpu.VMEM((4, ROWS, HEADS * D), BF),
+            dma((8,)),
+            dma((4,)),
+        ],
         compiler_params=pltpu.CompilerParams(vmem_limit_bytes=64 * 1024 * 1024),
         name="layout",
     )(heads, second, third, bias)

time: 39.9 us -> 40.3 us (1.010)
    pallas_call x1, Pallas kernels: 3.09 us -> 4.07 us  [paired(): pl.pallas_call(layout_kernel, out_shape=[jax.ShapeDtypeStruct((ROWS, HEAD...]
    pallas_call x1, Pallas kernels: 36.1 us -> 35.4 us  [paired(): pl.pallas_call(lambda *refs: main_kernel(ctx_count, dp_count, *refs), out...]
where the time goes in v4:
time: 40.3 us; the launch traced here: 40.1 us
  Pallas kernels  39.5 us (98%)
  between operations  0.64 us (2%)
    pallas_call x1, Pallas kernels, paired(): pl.pallas_call(lambda *refs: main_kernel(ctx_count, dp_count, *refs), out...  35.4 us
    pallas_call x1, Pallas kernels, paired(): pl.pallas_call(layout_kernel, out_shape=[jax.ShapeDtypeStruct((ROWS, HEAD...  4.07 us

profile of v4, /device:TPU:0, one launch (start us, length us, event | category | flops | bytes accessed | tf_op | source)
XLA Modules:
  0.0 40.1 jit_solution(10840225815610354946)
XLA Ops:
  0.6 35.4 %attend.1 = (bf16[8,2,256,128]{3,2,1,0:T(8,128)(2,1)}, f32[4,32,256]{2,1,0:T(8,128)}, f32[4,8,256]{2,1,0:T(8,128)}, f32[8,128]{1,0:T(8,128)}) custom-call(f32[2,32]{1,0:T(2,128)} %bitcast.14, s32[1,256]{1,0:T(1,128)} %refs_1_.1, bf16[256,1024]{1,0:T(8,128)(2,1)} %bitcast.10, bf16[256,1024]{1,0:T(8,128)(2,1)} %bitcast.11, bf16[256,1024]{1,0:T(8,128)(2,1)} %bitcast.12, ...), custom_call_target="tpu_custom_call" | custom-call | tf_op jit(solution)/shard_map/attend/pallas_call | solution.py:850
  36.0 4.1 %layout.1 = (bf16[256,1024]{1,0:T(8,128)(2,1)}, bf16[256,1024]{1,0:T(8,128)(2,1)}, bf16[256,1024]{1,0:T(8,128)(2,1)}, bf16[256,1024]{1,0:T(8,128)(2,1)}, f32[2,32]{1,0:T(2,128)}) custom-call(bf16[8,2,256,128]{3,2,1,0:T(8,128)(2,1)} %get-tuple-element.14.heads_hbm, f32[4,32,256]{2,1,0:T(8,128)} %get-tuple-element.15.second_ref, ...), custom_call_target="tpu_custom_call" | custom-call | tf_op jit(solution)/shard_map/layout/pallas_call | solution.py:906

commit v5 on v4

--- a/solution.py
+++ b/solution.py
@@ -408,20 +408,22 @@
         return pl.ds(pl.multiple_of(head * D, D), D)
 
     inputs = (k_ref, v_ref, q_ref, g_ref)
-    loads = [
-        pltpu.make_async_copy(ref.at[:, columns(head)], local.at[i, j], local_sem.at[3 * i + j])
+    parts = [
+        [
+            pltpu.make_async_copy(ref.at[:, columns(head)], local.at[j, i], local_sem.at[4 * j + i])
+            for i, ref in enumerate(inputs)
+        ]
+        for j, head in enumerate((c, 2, 3, 1 - c))
+    ]
+    sample_loads = [
+        pltpu.make_async_copy(ref.at[:, 4 * D :], sampled.at[i], local_sem.at[16 + i])
         for i, ref in enumerate(inputs)
-        for j, head in enumerate((c, 2, 3))
-    ]
-    sample_loads = [
-        pltpu.make_async_copy(ref.at[:, 4 * D :], sampled.at[i], local_sem.at[12 + i])
-        for i, ref in enumerate(inputs)
     ]
     small_loads = [
-        pltpu.make_async_copy(clause_hbm, clause_ref, local_sem.at[16]),
-        pltpu.make_async_copy(table_hbm, table_ref, local_sem.at[17]),
-    ]
-    for copy in sample_loads + small_loads + loads:
+        pltpu.make_async_copy(clause_hbm, clause_ref, local_sem.at[20]),
+        pltpu.make_async_copy(table_hbm, table_ref, local_sem.at[21]),
+    ]
+    for copy in parts[3] + parts[0][:2] + sample_loads + small_loads + parts[1] + parts[2] + parts[0][2:]:
         copy.start()
 
     barrier = pltpu.get_barrier_semaphore()
@@ -446,28 +448,27 @@
         )
 
     band_out = [
-        remote(inputs[i].at[:, columns(1 - c)], pair_buf.at[i], i, partner) for i in range(4)
+        remote(local.at[3, pl.ds(2 * i, 2)], pair_buf.at[pl.ds(2 * i, 2)], i, partner) for i in range(2)
     ]
     first_out = [
-        remote(inputs[i].at[:, columns(2 + h)], pair_buf.at[4 + 4 * h + i], 18 + 4 * h + i, partner)
-        for h in range(2)
-        for i in range(4)
+        remote(local.at[1 + h], pair_buf.at[pl.ds(4 + 4 * h, 4)], 2 + h, partner) for h in range(2)
     ]
     clause_out = remote(clause_hbm, pair_clause, 8, partner)
     own_halo = [
-        remote(k_ref.at[:, columns(c)], halo_buf.at[1, 0], 9, outward),
-        remote(v_ref.at[:, columns(c)], halo_buf.at[1, 1], 10, outward),
+        remote(local.at[0, pl.ds(0, 2)], halo_buf.at[1], 9, outward),
         remote(clause_hbm, halo_clause.at[1], 11, outward),
     ]
     far_halo = [
-        remote(pair_buf.at[0], halo_buf.at[0, 0], 12, beyond),
-        remote(pair_buf.at[1], halo_buf.at[0, 1], 13, beyond),
+        remote(pair_buf.at[pl.ds(0, 2)], halo_buf.at[0], 12, beyond),
         remote(pair_clause, halo_clause.at[0], 14, beyond),
     ]
 
     clause_out.start()
-    for copy in band_out[:2]:
-        copy.start()
+    for copy in parts[3][:2]:
+        copy.wait()
+    band_out[0].start()
+    for copy in parts[0][:2]:
+        copy.wait()
 
     @pl.when(has_out)
     def _():
@@ -503,8 +504,12 @@
         device_id_type=mesh_id,
     )
     third_pair.start()
-    for copy in band_out[2:] + first_out[:4]:
-        copy.start()
+    for copy in parts[3][2:]:
+        copy.wait()
+    band_out[1].start()
+    for copy in parts[1]:
+        copy.wait()
+    first_out[0].start()
 
     for copy in small_loads:
         copy.wait()
@@ -519,7 +524,6 @@
 
     clause_out.wait_recv()
     band_out[0].wait_recv()
-    band_out[1].wait_recv()
 
     @pl.when(has_beyond)
     def _():
@@ -576,9 +580,9 @@
     ]
     for copy in smalls:
         copy.start()
-    for copy in loads:
+    for copy in parts[2] + parts[0][2:]:
         copy.wait()
-    own = [local[i, 0] for i in range(4)]
+    own = [local[0, i] for i in range(4)]
     other = [pair_buf[0], pair_buf[1]]
     clauses = {"own": clause_ref, "other": pair_clause}
     cols = {name: clause_column(ref) for name, ref in clauses.items()}
@@ -671,10 +675,8 @@
         back_out.start()
 
     ret = [remote(ret_send.at[i], out_ref.at[i, c], 4 + i, partner) for i in range(4)]
-    for copy in first_out[4:]:
-        copy.start()
-    band_out[2].wait_recv()
-    band_out[3].wait_recv()
+    first_out[1].start()
+    band_out[1].wait_recv()
     other += [pair_buf[2], pair_buf[3]]
 
     @pl.when(has_beyond)
@@ -728,10 +730,9 @@
         bias_out.append(copy)
 
     def first_group(h):
-        for copy in first_out[4 * h : 4 * h + 4]:
-            copy.wait_recv()
+        first_out[h].wait_recv()
         k, v, q, g = [
-            jnp.concatenate([local[i, 1 + h], pair_buf[4 + 4 * h + i]], axis=0) for i in range(4)
+            jnp.concatenate([local[1 + h, i], pair_buf[4 + 4 * h + i]], axis=0) for i in range(4)
         ]
         pair_scores[...] = nt(q, k)
         pair_wg[...] = nt(g, v)
@@ -816,30 +817,18 @@
             copy.wait_send()
 
 
-def layout_kernel(heads_hbm, second_ref, third_ref, tile_ref, *refs):
-    outs, bias_ref, heads, full, in_sem, out_sem = refs[:4], refs[4], *refs[5:]
-    loads = [pltpu.make_async_copy(heads_hbm.at[i], heads.at[i], in_sem.at[i]) for i in range(8)]
-    stores = [pltpu.make_async_copy(full.at[i], outs[i], out_sem.at[i]) for i in range(4)]
-    for i in range(4):
-        loads[i].start()
-        loads[4 + i].start()
-    bias_ref[...] = tile_ref[0:2, 0:BUCKETS]
-    for i in range(4):
+def layout_kernel(heads_ref, second_ref, third_ref, tile_ref, *outs):
+    outs[4][...] = tile_ref[0:2, 0:BUCKETS]
+    for i, out in enumerate(outs[:4]):
         for h in range(2):
+            out[:, h * D : (h + 1) * D] = heads_ref[i, h]
+            out[:, (2 + h) * D : (3 + h) * D] = heads_ref[4 + i, h]
             seconds = second_ref[i, :, h * D : (h + 1) * D].astype(BF)
             spread = tn(selector(32, DILATION_SECOND, h * DILATION_SECOND // 2), seconds)
-            full[i, :, (4 + h) * D : (5 + h) * D] = spread.astype(BF)
+            out[:, (4 + h) * D : (5 + h) * D] = spread.astype(BF)
             thirds = third_ref[i, :, h * D : (h + 1) * D].astype(BF)
             spread = tn(selector(8, DILATION_THIRD, h * DILATION_THIRD // 2), thirds)
-            full[i, :, (6 + h) * D : (7 + h) * D] = spread.astype(BF)
-        loads[i].wait()
-        loads[4 + i].wait()
-        for h in range(2):
-            full[i, :, h * D : (h + 1) * D] = heads[i, h]
-            full[i, :, (2 + h) * D : (3 + h) * D] = heads[4 + i, h]
-        stores[i].start()
-    for copy in stores:
-        copy.wait()
+            out[:, (6 + h) * D : (7 + h) * D] = spread.astype(BF)
 
 
 def paired(ctx_count, dp_count, query, key, value, grad_out, clause, bias_table):
@@ -862,10 +851,10 @@
             pltpu.VMEM((4, 8, 2 * D), F32),
             pltpu.SMEM((2, BUCKETS), F32),
             pltpu.VMEM((1, ROWS), jnp.int32),
-            pltpu.VMEM((4, 3) + block, BF),
+            pltpu.VMEM((4, 4) + block, BF),
             pltpu.VMEM((4, ROWS, 4 * D), BF),
             pltpu.VMEM((12,) + block, BF),
-            dma((18,)),
+            dma((22,)),
             dma((14,)),
             pltpu.VMEM((12,) + block, BF),
             pltpu.VMEM((2, 2) + block, BF),
@@ -907,14 +896,8 @@
         layout_kernel,
         out_shape=[jax.ShapeDtypeStruct((ROWS, HEADS * D), BF)] * 4
         + [jax.ShapeDtypeStruct((2, BUCKETS), F32)],
-        in_specs=[far] + [vmem] * 3,
-        out_specs=[far] * 4 + [vmem],
-        scratch_shapes=[
-            pltpu.VMEM((8, 2) + block, BF),
-            pltpu.VMEM((4, ROWS, HEADS * D), BF),
-            dma((8,)),
-            dma((4,)),
-        ],
+        in_specs=[vmem] * 4,
+        out_specs=[vmem] * 5,
         compiler_params=pltpu.CompilerParams(vmem_limit_bytes=64 * 1024 * 1024),
         name="layout",
     )(heads, second, third, bias)

time: 40.3 us -> 39.3 us (0.975)
  Pallas kernels: 39.5 us -> 38.5 us
    pallas_call x1, Pallas kernels: 4.07 us -> 3.09 us  [paired(): pl.pallas_call(layout_kernel, out_shape=[jax.ShapeDtypeStruct((ROWS, HEAD...]
where the time goes in v5:
time: 39.3 us; the launch traced here: 39.1 us
  Pallas kernels  38.5 us (98%)
  between operations  0.64 us (2%)
    pallas_call x1, Pallas kernels, paired(): pl.pallas_call(lambda *refs: main_kernel(ctx_count, dp_count, *refs), out...  35.4 us
    pallas_call x1, Pallas kernels, paired(): pl.pallas_call(layout_kernel, out_shape=[jax.ShapeDtypeStruct((ROWS, HEAD...  3.09 us

profile of v5, /device:TPU:0, one launch (start us, length us, event | category | flops | bytes accessed | tf_op | source)
XLA Modules:
  0.0 39.1 jit_solution(14267808019144860888)
XLA Ops:
  0.6 35.4 %attend.1 = (bf16[8,2,256,128]{3,2,1,0:T(8,128)(2,1)}, f32[4,32,256]{2,1,0:T(8,128)}, f32[4,8,256]{2,1,0:T(8,128)}, f32[8,128]{1,0:T(8,128)}) custom-call(f32[2,32]{1,0:T(2,128)} %bitcast.14, s32[1,256]{1,0:T(1,128)} %refs_1_.1, bf16[256,1024]{1,0:T(8,128)(2,1)} %bitcast.10, bf16[256,1024]{1,0:T(8,128)(2,1)} %bitcast.11, bf16[256,1024]{1,0:T(8,128)(2,1)} %bitcast.12, ...), custom_call_target="tpu_custom_call" | custom-call | tf_op jit(solution)/shard_map/attend/pallas_call | solution.py:839
  36.1 3.1 %layout.1 = (bf16[256,1024]{1,0:T(8,128)(2,1)}, bf16[256,1024]{1,0:T(8,128)(2,1)}, bf16[256,1024]{1,0:T(8,128)(2,1)}, bf16[256,1024]{1,0:T(8,128)(2,1)}, f32[2,32]{1,0:T(2,128)}) custom-call(bf16[8,2,256,128]{3,2,1,0:T(8,128)(2,1)} %get-tuple-element.14.heads_ref, f32[4,32,256]{2,1,0:T(8,128)} %get-tuple-element.15.second_ref, ...), custom_call_target="tpu_custom_call" | custom-call | tf_op jit(solution)/shard_map/layout/pallas_call | solution.py:895

commit v6 on v5

--- a/solution.py
+++ b/solution.py
@@ -607,7 +607,7 @@
         reach = jnp.where(halo_valid, 0, ROWS)
         col = cols[mine_name]
         turn = (1 - 2 * c) * sign
-        chunk = 32
+        chunk = 16
 
         def near_clauses(start):
             return jnp.abs(col[start : start + chunk, 0:1] - key_row) < BUCKETS - 1
@@ -737,7 +737,7 @@
         pair_scores[...] = nt(q, k)
         pair_wg[...] = nt(g, v)
         softmax_rows(
-            2 * ROWS, 32, pair_scores, pair_wg, pair_w, pair_sg,
+            2 * ROWS, 16, pair_scores, pair_wg, pair_w, pair_sg,
             lambda at, start, scores: scores * scale, lambda at, logit_grads: None,
         )
         keep(4 + 4 * h, nn(pair_w[:ROWS, :], v))
@@ -818,17 +818,22 @@
 
 
 def layout_kernel(heads_ref, second_ref, third_ref, tile_ref, *outs):
+    half = ROWS // 2
     outs[4][...] = tile_ref[0:2, 0:BUCKETS]
+    first_row = pl.program_id(0) * half
+
+    def spread(ref, i, h, count, step, offset):
+        row = lax.broadcasted_iota(jnp.int32, (count, half), 0)
+        col = lax.broadcasted_iota(jnp.int32, (count, half), 1)
+        pick = (col + offset == row * step + h * step // 2).astype(BF)
+        return tn(pick, ref[i, :, h * D : (h + 1) * D].astype(BF)).astype(BF)
+
     for i, out in enumerate(outs[:4]):
         for h in range(2):
             out[:, h * D : (h + 1) * D] = heads_ref[i, h]
             out[:, (2 + h) * D : (3 + h) * D] = heads_ref[4 + i, h]
-            seconds = second_ref[i, :, h * D : (h + 1) * D].astype(BF)
-            spread = tn(selector(32, DILATION_SECOND, h * DILATION_SECOND // 2), seconds)
-            out[:, (4 + h) * D : (5 + h) * D] = spread.astype(BF)
-            thirds = third_ref[i, :, h * D : (h + 1) * D].astype(BF)
-            spread = tn(selector(8, DILATION_THIRD, h * DILATION_THIRD // 2), thirds)
-            out[:, (6 + h) * D : (7 + h) * D] = spread.astype(BF)
+            out[:, (4 + h) * D : (5 + h) * D] = spread(second_ref, i, h, 16, DILATION_SECOND, 0)
+            out[:, (6 + h) * D : (7 + h) * D] = spread(third_ref, i, h, 8, DILATION_THIRD, first_row)
 
 
 def paired(ctx_count, dp_count, query, key, value, grad_out, clause, bias_table):
@@ -896,8 +901,15 @@
         layout_kernel,
         out_shape=[jax.ShapeDtypeStruct((ROWS, HEADS * D), BF)] * 4
         + [jax.ShapeDtypeStruct((2, BUCKETS), F32)],
-        in_specs=[vmem] * 4,
-        out_specs=[vmem] * 5,
+        grid=(2,),
+        in_specs=[
+            pl.BlockSpec((8, 2, ROWS // 2, D), lambda i: (0, 0, i, 0)),
+            pl.BlockSpec((4, 16, 2 * D), lambda i: (0, i, 0)),
+            pl.BlockSpec((4, 8, 2 * D), lambda i: (0, 0, 0)),
+            pl.BlockSpec((8, D), lambda i: (0, 0)),
+        ],
+        out_specs=[pl.BlockSpec((ROWS // 2, HEADS * D), lambda i: (i, 0))] * 4
+        + [pl.BlockSpec((2, BUCKETS), lambda i: (0, 0))],
         compiler_params=pltpu.CompilerParams(vmem_limit_bytes=64 * 1024 * 1024),
         name="layout",
     )(heads, second, third, bias)

time: 39.3 us -> 39 us (level)
  no operation moved by 1% of the time
where the time goes in v6:
time: 39 us; the launch traced here: 38.8 us
  Pallas kernels  38.2 us (98%)
  between operations  0.64 us (2%)
    pallas_call x1, Pallas kernels, paired(): pl.pallas_call(lambda *refs: main_kernel(ctx_count, dp_count, *refs), out...  35.4 us
    pallas_call x1, Pallas kernels, paired(): pl.pallas_call(layout_kernel, out_shape=[jax.ShapeDtypeStruct((ROWS, HEAD...  2.77 us

profile of v6, /device:TPU:0, one launch (start us, length us, event | category | flops | bytes accessed | tf_op | source)
XLA Modules:
  0.0 38.8 jit_solution(2423704617794844208)
XLA Ops:
  0.6 35.4 %attend.1 = (bf16[8,2,256,128]{3,2,1,0:T(8,128)(2,1)}, f32[4,32,256]{2,1,0:T(8,128)}, f32[4,8,256]{2,1,0:T(8,128)}, f32[8,128]{1,0:T(8,128)}) custom-call(f32[2,32]{1,0:T(2,128)} %bitcast.14, s32[1,256]{1,0:T(1,128)} %refs_1_.1, bf16[256,1024]{1,0:T(8,128)(2,1)} %bitcast.10, bf16[256,1024]{1,0:T(8,128)(2,1)} %bitcast.11, bf16[256,1024]{1,0:T(8,128)(2,1)} %bitcast.12, ...), custom_call_target="tpu_custom_call" | custom-call | tf_op jit(solution)/shard_map/attend/pallas_call | solution.py:844
  36.1 2.8 %layout.1 = (bf16[256,1024]{1,0:T(8,128)(2,1)}, bf16[256,1024]{1,0:T(8,128)(2,1)}, bf16[256,1024]{1,0:T(8,128)(2,1)}, bf16[256,1024]{1,0:T(8,128)(2,1)}, f32[2,32]{1,0:T(2,128)}) custom-call(bf16[8,2,256,128]{3,2,1,0:T(8,128)(2,1)} %get-tuple-element.14.heads_ref, f32[4,32,256]{2,1,0:T(8,128)} %get-tuple-element.15.second_ref, ...), custom_call_target="tpu_custom_call" | custom-call | tf_op jit(solution)/shard_map/layout/pallas_call | solution.py:900
